TPU v7x, 128 devices: a whole 4x4x4 slice. The times are simulated.
128 devices in a mesh: grp: 4 (over z_hi, core), dev: 32 (over z_lo, x, y).
Axes of the slice: x: 4, y: 4, z: 4 (z_hi: 2, z_lo: 2; z = z_hi * 2 + z_lo), core: 2. Of those that a mesh axis runs over, the one named last changes fastest.
Arguments:
- images: bfloat16 [131072, 1152], P(('grp', 'dev')), may hold values from -60 to 60
- texts: bfloat16 [131072, 1152], P(('grp', 'dev')), may hold values from -60 to 60
- log_scale: float32 [1], replicated, may hold values from 1.6 to 2.6
- logit_bias: float32 [1], replicated, may hold values from -4 to -1
Outputs:
- grad_images: float32 [131072, 1152], P(('grp', 'dev'))
- grad_texts: float32 [131072, 1152], P(('grp', 'dev'))
All inputs are finite; a program needn't handle non-finite values.
Results may differ from a plain program's by a relative error of at most 0.004.
Values may be sent and summed in bfloat16 or wider, within the bound.
No kernel may reach another device: no remote copies, remote signals or barrier semaphores. Data moves between devices by JAX's collectives and lax.ppermute only.
A program may use at most 128 MiB of HBM per device.

v0:
```python
import jax
import jax.numpy as jnp
from jax import lax
from jax.sharding import PartitionSpec as P

epsilon = 1e-06


def passed_along(value, axis, steps):
    count = lax.axis_size(axis)
    pairs = [(source, (source + steps) % count) for source in range(count)]
    return lax.ppermute(value, axis, pairs)


def normalize(raw_rows):
    rows32 = raw_rows.astype(jnp.float32)
    inverse = lax.rsqrt(jnp.sum(rows32 * rows32, axis=1, keepdims=True) + epsilon)
    return (rows32 * inverse, inverse)


def pair_block(picture, caption, temper, offset, diagonal):
    logits = (
        temper
        * lax.dot_general(
            picture, caption, (((1,), (1,)), ((), ())), preferred_element_type=jnp.float32
        )
        + offset
    )
    weights = jax.nn.sigmoid(logits)
    if diagonal:
        across = lax.broadcasted_iota(jnp.int32, logits.shape, 0)
        down = lax.broadcasted_iota(jnp.int32, logits.shape, 1)
        weights = weights - jnp.where(across == down, 1.0, 0.0).astype(weights.dtype)
    weights_b = weights.astype(jnp.bfloat16)
    toward_img = jnp.dot(weights_b, caption, preferred_element_type=jnp.float32)
    toward_txt = lax.dot_general(
        weights_b, picture, (((0,), (0,)), ((), ())), preferred_element_type=jnp.float32
    )
    return (toward_img, toward_txt)


def project_back(unit_rows, grad_unit, inverse):
    along = jnp.sum(unit_rows * grad_unit, axis=1, keepdims=True)
    return (grad_unit - unit_rows * along) * inverse


def local(images, texts, log_scale, logit_bias):
    temper = jnp.exp(log_scale[0])
    offset = logit_bias[0]
    unit_img, inv_img = normalize(images)
    unit_txt, inv_txt = normalize(texts)
    picture = unit_img.astype(jnp.bfloat16)
    caption = unit_txt.astype(jnp.bfloat16)
    caption_near = passed_along(caption, ("grp", "dev"), 1)
    caption_far = passed_along(caption_near, ("grp", "dev"), 1)
    img_own, txt_own = pair_block(picture, caption, temper, offset, True)
    img_near, txt_near = pair_block(picture, caption_near, temper, offset, False)
    img_far, txt_far = pair_block(picture, caption_far, temper, offset, False)
    back_near = passed_along(txt_near, ("grp", "dev"), -1)
    back_far = passed_along(txt_far, ("grp", "dev"), -2)
    summed = txt_own + back_near + back_far
    grad_x = temper * (img_own + img_near + img_far)
    grad_y = temper * summed
    return (project_back(unit_img, grad_x, inv_img), project_back(unit_txt, grad_y, inv_txt))


def solution(mesh):
    return jax.shard_map(
        local,
        mesh=mesh,
        in_specs=(P(("grp", "dev"), None), P(("grp", "dev"), None), P(), P()),
        out_specs=(P(("grp", "dev"), None), P(("grp", "dev"), None)),
        check_vma=False,
    )
```

profile of v0, /device:TPU:16, one launch (start us, length us, event | category | flops | bytes accessed | tf_op | source)
XLA Modules:
  0.0 344.4 jit_solution(15022195896829327255)
XLA Ops:
  0.6 0.0 copy-start.1
  0.6 2.3 fusion.13
  3.0 2.1 fusion.2
  5.1 1.4 collective-permute-start
  6.5 51.7 %collective-permute-done = bf16[1024,1152]{1,0:T(8,128)(2,1)S(1)} collective-permute-done((bf16[1024,1152]{1,0:T(8,128)(2,1)S(1)}, bf16[1024,1152]{1,0:T(8,128)(2,1)S(1)}, u32[]{:S(2)}, u32[]{:S(2)}) %collective-permute-start) | collective-permute-done | bytes 2359328 | tf_op jit(solution)/shard_map/ppermute | solution.py:12
  58.2 1.3 collective-permute-start.1
  60.8 0.0 copy-done.1
  60.8 0.5 fusion.9
  61.4 3.8 %divide_convert_fusion.1 = bf16[1024,1024]{1,0:T(8,128)(2,1)S(1)} fusion(bf16[1024,1152]{1,0:T(8,128)(2,1)S(1)} %collective-permute-done, f32[]{:T(128)} %bitcast.16, f32[]{:T(128)} %bitcast, bf16[1024,1152]{1,0:T(8,128)(2,1)S(1)} %copy-done.1, f32[1024]{0:T(1024)S(1)} %add_rsqrt_fusion.1), kind=kOutput, calls=%fused_computation.21 | convolution fusion | flops 2425749504 | bytes 6819848 | tf_op jit(solution)/shard_map/dot_general | solution.py:24
  65.1 3.2 fusion.16
  68.3 0.8 collective-permute-start.2
  69.1 41.2 %collective-permute-done.1 = bf16[1024,1152]{1,0:T(8,128)(2,1)S(1)} collective-permute-done((bf16[1024,1152]{1,0:T(8,128)(2,1)S(1)}, bf16[1024,1152]{1,0:T(8,128)(2,1)S(1)}, u32[]{:S(2)}, u32[]{:S(2)}) %collective-permute-start.1) | collective-permute-done | bytes 2359328 | tf_op jit(solution)/shard_map/ppermute | solution.py:12
  110.3 3.8 %divide_convert_fusion = bf16[1024,1024]{1,0:T(8,128)(2,1)S(1)} fusion(bf16[1024,1152]{1,0:T(8,128)(2,1)S(1)} %collective-permute-done.1, f32[]{:T(128)} %bitcast.15, f32[]{:T(128)} %bitcast, bf16[1024,1152]{1,0:T(8,128)(2,1)S(1)} %copy-done.1, f32[1024]{0:T(1024)S(1)} %add_rsqrt_fusion.1), kind=kOutput, calls=%fused_computation.20 | convolution fusion | flops 2425749504 | bytes 6819848 | tf_op jit(solution)/shard_map/dot_general | solution.py:24
  114.1 0.0 copy-start.2
  114.1 1.3 copy-done.2
  115.4 3.1 fusion.14
  118.6 13.2 %collective-permute-start.3 = (f32[1024,1152]{1,0:T(8,128)S(1)}, f32[1024,1152]{1,0:T(8,128)S(1)}, u32[]{:S(2)}, u32[]{:S(2)}) collective-permute-start(f32[1024,1152]{1,0:T(8,128)S(1)} %fusion.14), channel_id=1, source_target_pairs={{0,126},{1,127},{2,0},{3,1},{4,2},{5,3},{6,4},{7,5},{8,6},{9,7},{1... | collective-permute-start | bytes 14155784 | tf_op jit(solution)/shard_map/ppermute | solution.py:12
  131.8 4.1 %subtract_convert_fusion = bf16[1024,1024]{1,0:T(8,128)(2,1)S(1)} fusion(bf16[1024,1152]{1,0:T(8,128)(2,1)S(1)} %fusion.2, f32[]{:T(128)} %bitcast.14, f32[]{:T(128)} %bitcast, bf16[1024,1152]{1,0:T(8,128)(2,1)S(1)} %copy-done.1, f32[1024]{0:T(1024)S(1)} %add_rsqrt_fusion.1), kind=kOutput, calls=%fused_computation.22 | convolution fusion | flops 2428895232 | bytes 6819848 | tf_op jit(solution)/shard_map/dot_general | solution.py:24
  135.8 4.5 %fusion.22 = f32[1024,1152]{1,0:T(8,128)} fusion(bf16[1024,1024]{1,0:T(8,128)(2,1)S(1)} %subtract_convert_fusion, bf16[1024,1152]{1,0:T(8,128)(2,1)S(1)} %fusion.2), kind=kOutput, calls=%fused_computation.28 | convolution fusion | flops 2415919104 | bytes 9175040 | tf_op jit(solution)/shard_map/dot_general | solution.py:35
  140.3 4.5 %fusion.23 = f32[1024,1152]{1,0:T(8,128)} fusion(bf16[1024,1024]{1,0:T(8,128)(2,1)S(1)} %divide_convert_fusion.1, bf16[1024,1152]{1,0:T(8,128)(2,1)S(1)} %collective-permute-done), kind=kOutput, calls=%fused_computation.29 | convolution fusion | flops 2415919104 | bytes 9175040 | tf_op jit(solution)/shard_map/dot_general | solution.py:35
  144.8 7.7 %fusion.6 = (f32[1024]{0:T(1024)S(1)}, f32[1024,1152]{1,0:T(8,128)S(1)}) fusion(bf16[1024,1152]{1,0:T(8,128)(2,1)S(1)} %copy-done.1, f32[1024]{0:T(1024)S(1)} %add_rsqrt_fusion.1, bf16[1024,1024]{1,0:T(8,128)(2,1)} %copy-done.2, bf16[1024,1152]{1,0:T(8,128)(2,1)S(1)} %collective-permute-done.1, f32[1024,1152]{1,0:T(8,128)} %fusion.22, ...), kind=kOutput, calls=%fused_computation.10 | convolution fusion | flops 2424175616 | bytes 20979716 | tf_op jit(solution)/shard_map/dot_general | solution.py:35
  152.5 0.0 copy-start
  152.5 3.1 fusion.8
  155.6 18.8 %collective-permute-done.2 = f32[1024,1152]{1,0:T(8,128)S(1)} collective-permute-done((f32[1024,1152]{1,0:T(8,128)S(1)}, f32[1024,1152]{1,0:T(8,128)S(1)}, u32[]{:S(2)}, u32[]{:S(2)}) %collective-permute-start.2) | collective-permute-done | bytes 4718624 | tf_op jit(solution)/shard_map/ppermute | solution.py:12
  174.4 162.6 %collective-permute-done.3 = f32[1024,1152]{1,0:T(8,128)S(1)} collective-permute-done((f32[1024,1152]{1,0:T(8,128)S(1)}, f32[1024,1152]{1,0:T(8,128)S(1)}, u32[]{:S(2)}, u32[]{:S(2)}) %collective-permute-start.3) | collective-permute-done | bytes 4718624 | tf_op jit(solution)/shard_map/ppermute | solution.py:12
  337.0 0.0 copy-done
  337.0 4.3 %fusion.10 = (f32[1024]{0:T(1024)S(1)}, f32[1024,1152]{1,0:T(8,128)S(1)}) fusion(bf16[1024,1152]{1,0:T(8,128)(2,1)S(1)} %copy-done, f32[1024]{0:T(1024)S(1)} %add_rsqrt_fusion, f32[1024,1152]{1,0:T(8,128)S(1)} %collective-permute-done.3, f32[1024,1152]{1,0:T(8,128)S(1)} %collective-permute-done.2, bf16[1024,1024]{1,0:T(8,128)(2,1)S(1)} %subtract_convert_fusion, ...), kind=kOutput, calls=%fused_computation.14 | convolution fusion | flops 2427714560 | bytes 20983812 | tf_op jit(solution)/shard_map/dot_general | solution.py:36
  341.3 3.1 fusion.12
  (2 shorter events, 0.0 us)
Async XLA Ops:
  0.6 60.2 %copy-start.1 = (bf16[1024,1152]{1,0:T(8,128)(2,1)S(1)}, bf16[1024,1152]{1,0:T(8,128)(2,1)}, u32[]{:S(2)}) copy-start(bf16[1024,1152]{1,0:T(8,128)(2,1)} %param.4) | copy-start | bytes 7077892
  5.1 53.1 %collective-permute-start = (bf16[1024,1152]{1,0:T(8,128)(2,1)S(1)}, bf16[1024,1152]{1,0:T(8,128)(2,1)S(1)}, u32[]{:S(2)}, u32[]{:S(2)}) collective-permute-start(bf16[1024,1152]{1,0:T(8,128)(2,1)S(1)} %fusion.2), channel_id=1, source_target_pairs={{0,1},{1,2},{2,3},{3,4},{4,5},{5,6},{6,7},{7,8},{8,9},{9,10},{10,1... | collective-permute-start | bytes 7077896 | tf_op jit(solution)/shard_map/ppermute | solution.py:12
  58.2 52.1 %collective-permute-start.1 = (bf16[1024,1152]{1,0:T(8,128)(2,1)S(1)}, bf16[1024,1152]{1,0:T(8,128)(2,1)S(1)}, u32[]{:S(2)}, u32[]{:S(2)}) collective-permute-start(bf16[1024,1152]{1,0:T(8,128)(2,1)S(1)} %collective-permute-done), channel_id=1, source_target_pairs={{0,1},{1,2},{2,3},{3,4},{4,5},{5,6},{6,7},{7,8},{8,9},{9,10},{10,1... | collective-permute-start | bytes 7077896 | tf_op jit(solution)/shard_map/ppermute | solution.py:12
  68.3 106.1 %collective-permute-start.2 = (f32[1024,1152]{1,0:T(8,128)S(1)}, f32[1024,1152]{1,0:T(8,128)S(1)}, u32[]{:S(2)}, u32[]{:S(2)}) collective-permute-start(f32[1024,1152]{1,0:T(8,128)S(1)} %fusion.16), channel_id=1, source_target_pairs={{0,127},{1,0},{2,1},{3,2},{4,3},{5,4},{6,5},{7,6},{8,7},{9,8},{10,... | collective-permute-start | bytes 14155784 | tf_op jit(solution)/shard_map/ppermute | solution.py:12
  114.1 1.4 copy-start.2
  118.6 218.4 %collective-permute-start.3 = (f32[1024,1152]{1,0:T(8,128)S(1)}, f32[1024,1152]{1,0:T(8,128)S(1)}, u32[]{:S(2)}, u32[]{:S(2)}) collective-permute-start(f32[1024,1152]{1,0:T(8,128)S(1)} %fusion.14), channel_id=1, source_target_pairs={{0,126},{1,127},{2,0},{3,1},{4,2},{5,3},{6,4},{7,5},{8,6},{9,7},{1... | collective-permute-start | bytes 14155784 | tf_op jit(solution)/shard_map/ppermute | solution.py:12
  152.5 184.5 %copy-start = (bf16[1024,1152]{1,0:T(8,128)(2,1)S(1)}, bf16[1024,1152]{1,0:T(8,128)(2,1)}, u32[]{:S(2)}) copy-start(bf16[1024,1152]{1,0:T(8,128)(2,1)} %param.5) | copy-start | bytes 7077892
where the time goes:
time: 345 us; the launch traced here: 344 us
  waiting for transfers between devices  274 us (79%)
  matrix products  38.9 us (11%)
  starting transfers between devices  16.6 us (5%)
  other arithmetic  11.1 us (3%)
    ppermute x4, waiting for transfers between devices, passed_along(): return lax.ppermute(value, axis, pairs)  274 us
    dot_general x3, matrix products, pair_block(): toward_img = jnp.dot(weights_b, caption, preferred_element_type=jnp.float32)  16.7 us
    ppermute x4, starting transfers between devices, passed_along(): return lax.ppermute(value, axis, pairs)  16.6 us
    dot_general x3, matrix products, pair_block(): lax.dot_general(picture, caption, (((1,), (1,)), ((), ())), preferred_ele...  11.6 us
    dot_general x3, matrix products, pair_block(): lax.dot_general(weights_b, picture, (((0,), (0,)), ((), ())), preferred_e...  10.6 us
  transfers between devices with their start and end apart: 4, of which 4 were waited for; matrix products, arithmetic and copies ran while one was open for 11% of the time, Pallas kernels for 0%

commit v1 on v0

v1 whole, which is shorter than its diff:
```python
import functools

import jax
import jax.numpy as jnp
from jax import lax
from jax.experimental import pallas as pl
from jax.experimental.pallas import tpu as pltpu
from jax.sharding import PartitionSpec as P

epsilon = 1e-06
axes = ("grp", "dev")
cuts = (0, 768, 1024)
tile = 256


def passed_along(value, steps):
    count = lax.axis_size(axes)
    pairs = [(source, (source + steps) % count) for source in range(count)]
    return lax.ppermute(value, axes, pairs)


def normalize(raw_rows):
    rows32 = raw_rows.astype(jnp.float32)
    inverse = lax.rsqrt(jnp.sum(rows32 * rows32, axis=1, keepdims=True) + epsilon)
    return rows32 * inverse, inverse


def project_back(unit_rows, grad_unit, inverse):
    along = jnp.sum(unit_rows * grad_unit, axis=1, keepdims=True)
    return (grad_unit - unit_rows * along) * inverse


def attend(own, others, temper, offset, first_row):
    logits = (
        temper
        * lax.dot_general(own, others, (((1,), (1,)), ((), ())), preferred_element_type=jnp.float32)
        + offset
    )
    weights = jax.nn.sigmoid(logits)
    if first_row is not None:
        across = lax.broadcasted_iota(jnp.int32, logits.shape, 0) + first_row
        down = lax.broadcasted_iota(jnp.int32, logits.shape, 1)
        weights = weights - jnp.where(across == down, 1.0, 0.0)
    return jnp.dot(weights.astype(jnp.bfloat16), others, preferred_element_type=jnp.float32)


def kernel(pieces, diagonal, last, temper_ref, offset_ref, *refs):
    img_ref, txt_ref = refs[:2]
    txt_pieces, img_pieces = refs[2 : 2 + pieces], refs[2 + pieces : 2 + 2 * pieces]
    rest = refs[2 + 2 * pieces :]
    if not diagonal:
        (gx_ref, gy_ref), rest = rest[:2], rest[2:]
    out_x, out_y, txt_unit, img_unit = rest
    step = pl.program_id(0)
    temper, offset = temper_ref[0], offset_ref[0]

    @pl.when(step == 0)
    def _():
        for piece_refs, unit_ref in ((txt_pieces, txt_unit), (img_pieces, img_unit)):
            at = 0
            for piece in piece_refs:
                for start in range(0, piece.shape[0], 128):
                    unit, _ = normalize(piece[start : start + 128])
                    unit_ref[at : at + 128] = unit.astype(jnp.bfloat16)
                    at += 128

    first_row = step * tile if diagonal else None
    sides = ((img_ref, txt_unit, out_x), (txt_ref, img_unit, out_y))
    for side, (own_ref, others, out) in enumerate(sides):
        unit, inverse = normalize(own_ref[...])
        total = attend(unit.astype(jnp.bfloat16), others[...], temper, offset, first_row)
        if not diagonal:
            total = total + (gx_ref, gy_ref)[side][...]
        if last:
            total = project_back(unit, temper * total, inverse)
        out[...] = total


def block_sums(temper, offset, images, texts, txt_pieces, img_pieces, sums, last):
    rows, width = images.shape
    pieces = len(txt_pieces)
    others = sum(piece.shape[0] for piece in txt_pieces)
    scalar = pl.BlockSpec(memory_space=pltpu.SMEM)
    rows_spec = pl.BlockSpec((tile, width), lambda i: (i, 0))
    whole = [pl.BlockSpec(piece.shape, lambda i: (0, 0)) for piece in txt_pieces]
    diagonal = not sums
    return pl.pallas_call(
        functools.partial(kernel, pieces, diagonal, last),
        grid=(rows // tile,),
        in_specs=[scalar, scalar, rows_spec, rows_spec] + whole * 2 + [rows_spec] * len(sums),
        out_specs=[rows_spec] * 2,
        out_shape=[jax.ShapeDtypeStruct((rows, width), jnp.float32)] * 2,
        scratch_shapes=[pltpu.VMEM((others, width), jnp.bfloat16)] * 2,
        compiler_params=pltpu.CompilerParams(vmem_limit_bytes=40 * 2**20),
        cost_estimate=pl.CostEstimate(
            flops=8 * rows * others * width, bytes_accessed=16 * rows * width, transcendentals=0
        ),
    )(temper, offset, images, texts, *txt_pieces, *img_pieces, *sums)


def local(images, texts, log_scale, logit_bias):
    temper = jnp.exp(log_scale)
    near_txt, near_img, far_txt, far_img = [], [], [], []
    for low, high in zip(cuts, cuts[1:]):
        near_txt.append(passed_along(texts[low:high], 1))
        near_img.append(passed_along(images[low:high], -1))
    for txt, img in zip(near_txt, near_img):
        far_txt.append(passed_along(txt, 1))
        far_img.append(passed_along(img, -1))
    blocks = functools.partial(block_sums, temper, logit_bias, images, texts)
    sums = blocks([texts], [images], (), False)
    sums = blocks(near_txt, near_img, sums, False)
    sums = blocks(far_txt[:1], far_img[:1], sums, False)
    return tuple(blocks(far_txt[1:], far_img[1:], sums, True))


def solution(mesh):
    return jax.shard_map(
        local,
        mesh=mesh,
        in_specs=(P(axes, None), P(axes, None), P(), P()),
        out_specs=(P(axes, None), P(axes, None)),
        check_vma=False,
    )
```

time: 345 us -> 127 us (0.37)
  the two profiles are of different devices: /device:TPU:16 before, /device:TPU:0 now
where the time goes in v1:
time: 127 us
  Pallas kernels  55.8 us (44%)
  starting transfers between devices  30.5 us (24%)
  waiting for transfers between devices  30.3 us (24%)
  local copies, waits for them, and re-layouts  8.55 us (7%)
  between operations  2.05 us (2%)
    pallas_call x4, Pallas kernels, block_sums(): pl.pallas_call(functools.partial(kernel, pieces, diagonal, last), grid=(r...  55.8 us
    ppermute x8, starting transfers between devices, passed_along(): return lax.ppermute(value, axes, pairs)  30.5 us
    ppermute x8, waiting for transfers between devices, passed_along(): return lax.ppermute(value, axes, pairs)  30.3 us
    unnamed x10, local copies, waits for them, and re-layouts  6.56 us
  transfers between devices with their start and end apart: 8, of which 2 were waited for; matrix products, arithmetic and copies ran while one was open for 0% of the time, Pallas kernels for 35%

profile of v1, /device:TPU:0, one launch (start us, length us, event | category | flops | bytes accessed | tf_op | source)
XLA Modules:
  0.0 127.2 jit_solution(17224245616732786734)
XLA Ops:
  0.6 0.0 copy-start
  0.6 0.0 copy-start.1
  0.6 1.8 %slice.14 = bf16[768,1152]{1,0:T(8,128)(2,1)S(1)} slice(bf16[1024,1152]{1,0:T(8,128)(2,1)} %refs_1_.7), slice={[0:768], [0:1152]} | slice | bytes 3538944 | tf_op jit(solution)/shard_map/slice | solution.py:105
  2.4 1.7 %collective-permute-start.4 = (bf16[768,1152]{1,0:T(8,128)(2,1)S(1)}, bf16[768,1152]{1,0:T(8,128)(2,1)S(1)}, u32[]{:S(2)}, u32[]{:S(2)}) collective-permute-start(bf16[768,1152]{1,0:T(8,128)(2,1)S(1)} %slice.14), channel_id=1, source_target_pairs={{0,1},{1,2},{2,3},{3,4},{4,5},{5,6},{6,7},{7,8},{8,9},{9,10},{10,1... | collective-permute-start | bytes 5308424 | tf_op jit(solution)/shard_map/ppermute | solution.py:19
  4.1 0.0 copy-done
  4.2 0.1 slice.15
  4.3 7.0 %collective-permute-start.6 = (bf16[768,1152]{1,0:T(8,128)(2,1)S(1)}, bf16[768,1152]{1,0:T(8,128)(2,1)S(1)}, u32[]{:S(2)}, u32[]{:S(2)}) collective-permute-start(bf16[768,1152]{1,0:T(8,128)(2,1)S(1)} %slice.15), channel_id=1, source_target_pairs={{0,127},{1,0},{2,1},{3,2},{4,3},{5,4},{6,5},{7,6},{8,7},{9,8},{10,... | collective-permute-start | bytes 5308424 | tf_op jit(solution)/shard_map/ppermute | solution.py:19
  11.2 0.0 copy-done.1
  11.3 0.1 collective-permute-start
  11.4 7.2 %collective-permute-start.2 = (bf16[256,1152]{1,0:T(8,128)(2,1)S(1)}, bf16[256,1152]{1,0:T(8,128)(2,1)S(1)}, u32[]{:S(2)}, u32[]{:S(2)}) collective-permute-start(bf16[256,1152]{1,0:T(8,128)(2,1)S(1)} %slice.13), channel_id=1, source_target_pairs={{0,127},{1,0},{2,1},{3,2},{4,3},{5,4},{6,5},{7,6},{8,7},{9,8},{10,... | collective-permute-start | bytes 1769480 | tf_op jit(solution)/shard_map/ppermute | solution.py:19
  20.0 29.0 %collective-permute-done.4.refs_2_ = bf16[768,1152]{1,0:T(8,128)(2,1)S(1)} collective-permute-done((bf16[768,1152]{1,0:T(8,128)(2,1)S(1)}, bf16[768,1152]{1,0:T(8,128)(2,1)S(1)}, u32[]{:S(2)}, u32[]{:S(2)}) %collective-permute-start.4) | collective-permute-done | bytes 1769504 | tf_op jit(solution)/shard_map/ppermute | solution.py:19
  49.0 0.0 collective-permute-start.5
  49.0 1.3 %collective-permute-done.6.refs_4_ = bf16[768,1152]{1,0:T(8,128)(2,1)S(1)} collective-permute-done((bf16[768,1152]{1,0:T(8,128)(2,1)S(1)}, bf16[768,1152]{1,0:T(8,128)(2,1)S(1)}, u32[]{:S(2)}, u32[]{:S(2)}) %collective-permute-start.6) | collective-permute-done | bytes 1769504 | tf_op jit(solution)/shard_map/ppermute | solution.py:19
  50.3 7.3 %collective-permute-start.7 = (bf16[768,1152]{1,0:T(8,128)(2,1)S(1)}, bf16[768,1152]{1,0:T(8,128)(2,1)S(1)}, u32[]{:S(2)}, u32[]{:S(2)}) collective-permute-start(bf16[768,1152]{1,0:T(8,128)(2,1)S(1)} %collective-permute-done.6.refs_4_), channel_id=1, source_target_pairs={{0,127},{1,0},{2,1},{3,2},{4,3},{5,4},{6,5},{7,6},{8,7},{9,8},{10,... | collective-permute-start | bytes 5308424 | tf_op jit(solution)/shard_map/ppermute | solution.py:19
  57.6 13.8 %shard_map.59 = (f32[1024,1152]{1,0:T(8,128)S(1)}, f32[1024,1152]{1,0:T(8,128)S(1)}) custom-call(f32[1]{0:T(128)S(6)} %exp.3.temper_ref, f32[1]{0:T(128)S(6)} %copy.7.offset_ref, bf16[1024,1152]{1,0:T(8,128)(2,1)S(1)} %copy-done, bf16[1024,1152]{1,0:T(8,128)(2,1)S(1)} %copy-done.1, bf16[1024,1152]{1,0:T(8,128)(2,1)S(1)} %copy-done.1, ...), custom_call_target="tpu_custom_call" | custom-call | flops 9663676416 | bytes 18874368 | tf_op jit(solution)/shard_map/pallas_call | solution.py:87
  71.4 0.0 copy-start.3
  71.4 2.2 %copy-done.3 = f32[1024,1152]{1,0:T(8,128)} copy-done((f32[1024,1152]{1,0:T(8,128)}, f32[1024,1152]{1,0:T(8,128)S(1)}, u32[]{:S(2)}) %copy-start.3) | copy-done | bytes 4718616
  73.6 0.0 copy-start.4
  73.6 2.2 %copy-done.4 = f32[1024,1152]{1,0:T(8,128)} copy-done((f32[1024,1152]{1,0:T(8,128)}, f32[1024,1152]{1,0:T(8,128)S(1)}, u32[]{:S(2)}) %copy-start.4) | copy-done | bytes 4718616
  75.8 0.0 collective-permute-done.refs_3_
  75.8 0.0 collective-permute-start.1
  75.8 0.0 collective-permute-done.2.refs_5_
  75.8 7.2 %collective-permute-start.3 = (bf16[256,1152]{1,0:T(8,128)(2,1)S(1)}, bf16[256,1152]{1,0:T(8,128)(2,1)S(1)}, u32[]{:S(2)}, u32[]{:S(2)}) collective-permute-start(bf16[256,1152]{1,0:T(8,128)(2,1)S(1)} %collective-permute-done.2.refs_5_), channel_id=1, source_target_pairs={{0,127},{1,0},{2,1},{3,2},{4,3},{5,4},{6,5},{7,6},{8,7},{9,8},{10,... | collective-permute-start | bytes 1769480 | tf_op jit(solution)/shard_map/ppermute | solution.py:19
  83.0 16.3 %shard_map.60 = (f32[1024,1152]{1,0:T(8,128)S(1)}, f32[1024,1152]{1,0:T(8,128)}) custom-call(f32[1]{0:T(128)S(6)} %exp.3.temper_ref, f32[1]{0:T(128)S(6)} %copy.7.offset_ref, bf16[1024,1152]{1,0:T(8,128)(2,1)S(1)} %copy-done, bf16[1024,1152]{1,0:T(8,128)(2,1)S(1)} %copy-done.1, bf16[768,1152]{1,0:T(8,128)(2,1)S(1)} %collective-permute-done.4.refs_2_, ...), custom_call_target="tpu_custom_call" | custom-call | flops 9663676416 | bytes 18874368 | tf_op jit(solution)/shard_map/pallas_call | solution.py:87
  99.3 0.0 copy-start.2
  99.3 2.2 %copy-done.2 = f32[1024,1152]{1,0:T(8,128)} copy-done((f32[1024,1152]{1,0:T(8,128)}, f32[1024,1152]{1,0:T(8,128)S(1)}, u32[]{:S(2)}) %copy-start.2) | copy-done | bytes 4718616
  101.5 0.0 collective-permute-done.5.refs_2_
  101.5 0.0 collective-permute-done.7.refs_3_
  101.5 14.4 %shard_map.61 = (f32[1024,1152]{1,0:T(8,128)S(1)}, f32[1024,1152]{1,0:T(8,128)}) custom-call(f32[1]{0:T(128)S(6)} %exp.3.temper_ref, f32[1]{0:T(128)S(6)} %copy.7.offset_ref, bf16[1024,1152]{1,0:T(8,128)(2,1)S(1)} %copy-done, bf16[1024,1152]{1,0:T(8,128)(2,1)S(1)} %copy-done.1, bf16[768,1152]{1,0:T(8,128)(2,1)S(1)} %collective-permute-done.5.refs_2_, ...), custom_call_target="tpu_custom_call" | custom-call | flops 7247757312 | bytes 18874368 | tf_op jit(solution)/shard_map/pallas_call | solution.py:87
  115.9 0.0 collective-permute-done.1.refs_2_
  115.9 0.0 collective-permute-done.3.refs_3_
  115.9 11.3 %shard_map.62 = (f32[1024,1152]{1,0:T(8,128)}, f32[1024,1152]{1,0:T(8,128)}) custom-call(f32[1]{0:T(128)S(6)} %exp.3.temper_ref, f32[1]{0:T(128)S(6)} %copy.7.offset_ref, bf16[1024,1152]{1,0:T(8,128)(2,1)S(1)} %copy-done, bf16[1024,1152]{1,0:T(8,128)(2,1)S(1)} %copy-done.1, bf16[256,1152]{1,0:T(8,128)(2,1)S(1)} %collective-permute-done.1.refs_2_, ...), custom_call_target="tpu_custom_call" | custom-call | flops 2415919104 | bytes 18874368 | tf_op jit(solution)/shard_map/pallas_call | solution.py:87
  (2 shorter events, 0.1 us)
Async XLA Ops:
  0.6 3.5 %copy-start = (bf16[1024,1152]{1,0:T(8,128)(2,1)S(1)}, bf16[1024,1152]{1,0:T(8,128)(2,1)}, u32[]{:S(2)}) copy-start(bf16[1024,1152]{1,0:T(8,128)(2,1)} %refs_0_.7) | copy-start | bytes 7077892
  0.6 10.6 %copy-start.1 = (bf16[1024,1152]{1,0:T(8,128)(2,1)S(1)}, bf16[1024,1152]{1,0:T(8,128)(2,1)}, u32[]{:S(2)}) copy-start(bf16[1024,1152]{1,0:T(8,128)(2,1)} %refs_1_.7) | copy-start | bytes 7077892
  2.4 46.6 %collective-permute-start.4 = (bf16[768,1152]{1,0:T(8,128)(2,1)S(1)}, bf16[768,1152]{1,0:T(8,128)(2,1)S(1)}, u32[]{:S(2)}, u32[]{:S(2)}) collective-permute-start(bf16[768,1152]{1,0:T(8,128)(2,1)S(1)} %slice.14), channel_id=1, source_target_pairs={{0,1},{1,2},{2,3},{3,4},{4,5},{5,6},{6,7},{7,8},{8,9},{9,10},{10,1... | collective-permute-start | bytes 5308424 | tf_op jit(solution)/shard_map/ppermute | solution.py:19
  4.3 46.0 %collective-permute-start.6 = (bf16[768,1152]{1,0:T(8,128)(2,1)S(1)}, bf16[768,1152]{1,0:T(8,128)(2,1)S(1)}, u32[]{:S(2)}, u32[]{:S(2)}) collective-permute-start(bf16[768,1152]{1,0:T(8,128)(2,1)S(1)} %slice.15), channel_id=1, source_target_pairs={{0,127},{1,0},{2,1},{3,2},{4,3},{5,4},{6,5},{7,6},{8,7},{9,8},{10,... | collective-permute-start | bytes 5308424 | tf_op jit(solution)/shard_map/ppermute | solution.py:19
  11.3 64.5 %collective-permute-start = (bf16[256,1152]{1,0:T(8,128)(2,1)S(1)}, bf16[256,1152]{1,0:T(8,128)(2,1)S(1)}, u32[]{:S(2)}, u32[]{:S(2)}) collective-permute-start(bf16[256,1152]{1,0:T(8,128)(2,1)S(1)} %slice.12), channel_id=1, source_target_pairs={{0,1},{1,2},{2,3},{3,4},{4,5},{5,6},{6,7},{7,8},{8,9},{9,10},{10,1... | collective-permute-start | bytes 1769480 | tf_op jit(solution)/shard_map/ppermute | solution.py:19
  11.4 64.4 %collective-permute-start.2 = (bf16[256,1152]{1,0:T(8,128)(2,1)S(1)}, bf16[256,1152]{1,0:T(8,128)(2,1)S(1)}, u32[]{:S(2)}, u32[]{:S(2)}) collective-permute-start(bf16[256,1152]{1,0:T(8,128)(2,1)S(1)} %slice.13), channel_id=1, source_target_pairs={{0,127},{1,0},{2,1},{3,2},{4,3},{5,4},{6,5},{7,6},{8,7},{9,8},{10,... | collective-permute-start | bytes 1769480 | tf_op jit(solution)/shard_map/ppermute | solution.py:19
  49.0 52.5 %collective-permute-start.5 = (bf16[768,1152]{1,0:T(8,128)(2,1)S(1)}, bf16[768,1152]{1,0:T(8,128)(2,1)S(1)}, u32[]{:S(2)}, u32[]{:S(2)}) collective-permute-start(bf16[768,1152]{1,0:T(8,128)(2,1)S(1)} %collective-permute-done.4.refs_2_), channel_id=1, source_target_pairs={{0,1},{1,2},{2,3},{3,4},{4,5},{5,6},{6,7},{7,8},{8,9},{9,10},{10,1... | collective-permute-start | bytes 5308424 | tf_op jit(solution)/shard_map/ppermute | solution.py:19
  50.3 51.2 %collective-permute-start.7 = (bf16[768,1152]{1,0:T(8,128)(2,1)S(1)}, bf16[768,1152]{1,0:T(8,128)(2,1)S(1)}, u32[]{:S(2)}, u32[]{:S(2)}) collective-permute-start(bf16[768,1152]{1,0:T(8,128)(2,1)S(1)} %collective-permute-done.6.refs_4_), channel_id=1, source_target_pairs={{0,127},{1,0},{2,1},{3,2},{4,3},{5,4},{6,5},{7,6},{8,7},{9,8},{10,... | collective-permute-start | bytes 5308424 | tf_op jit(solution)/shard_map/ppermute | solution.py:19
  71.4 2.2 %copy-start.3 = (f32[1024,1152]{1,0:T(8,128)}, f32[1024,1152]{1,0:T(8,128)S(1)}, u32[]{:S(2)}) copy-start(f32[1024,1152]{1,0:T(8,128)S(1)} %get-tuple-element.8.refs_6_) | copy-start | bytes 14155780
  73.6 2.2 %copy-start.4 = (f32[1024,1152]{1,0:T(8,128)}, f32[1024,1152]{1,0:T(8,128)S(1)}, u32[]{:S(2)}) copy-start(f32[1024,1152]{1,0:T(8,128)S(1)} %get-tuple-element.9.refs_7_) | copy-start | bytes 14155780
  75.8 40.1 %collective-permute-start.1 = (bf16[256,1152]{1,0:T(8,128)(2,1)S(1)}, bf16[256,1152]{1,0:T(8,128)(2,1)S(1)}, u32[]{:S(2)}, u32[]{:S(2)}) collective-permute-start(bf16[256,1152]{1,0:T(8,128)(2,1)S(1)} %collective-permute-done.refs_3_), channel_id=1, source_target_pairs={{0,1},{1,2},{2,3},{3,4},{4,5},{5,6},{6,7},{7,8},{8,9},{9,10},{10,1... | collective-permute-start | bytes 1769480 | tf_op jit(solution)/shard_map/ppermute | solution.py:19
  75.8 40.1 %collective-permute-start.3 = (bf16[256,1152]{1,0:T(8,128)(2,1)S(1)}, bf16[256,1152]{1,0:T(8,128)(2,1)S(1)}, u32[]{:S(2)}, u32[]{:S(2)}) collective-permute-start(bf16[256,1152]{1,0:T(8,128)(2,1)S(1)} %collective-permute-done.2.refs_5_), channel_id=1, source_target_pairs={{0,127},{1,0},{2,1},{3,2},{4,3},{5,4},{6,5},{7,6},{8,7},{9,8},{10,... | collective-permute-start | bytes 1769480 | tf_op jit(solution)/shard_map/ppermute | solution.py:19
  99.3 2.2 %copy-start.2 = (f32[1024,1152]{1,0:T(8,128)}, f32[1024,1152]{1,0:T(8,128)S(1)}, u32[]{:S(2)}) copy-start(f32[1024,1152]{1,0:T(8,128)S(1)} %get-tuple-element.10.refs_4_) | copy-start | bytes 14155780

commit v2 on v0

v2 whole, which is shorter than its diff:
```python
import functools

import jax
import jax.numpy as jnp
from jax import lax
from jax.experimental import pallas as pl
from jax.experimental.pallas import tpu as pltpu
from jax.sharding import PartitionSpec as P


epsilon = 1e-06
axes = ("grp", "dev")
split = 768
tile = 256
lanes = 128


def exchanged(value, inner):
    count = lax.axis_size(axes)
    first = 0 if inner else 1
    pairs = []
    for low in range(first, count, 2):
        high = (low + 1) % count
        pairs += [(low, high), (high, low)]
    return lax.ppermute(value, axes, pairs)


def on_even(is_even, is_odd):
    odd = lax.rem(lax.axis_index("dev"), 2)
    pl.when(odd == 0)(is_even)
    pl.when(odd == 1)(is_odd)


def normalize(raw_rows):
    rows32 = raw_rows.astype(jnp.float32)
    inverse = lax.rsqrt(jnp.sum(rows32 * rows32, axis=1, keepdims=True) + epsilon)
    return rows32 * inverse, inverse


def unit_rows(pieces, unit_ref):
    base = 0
    for piece in pieces:
        for start in range(0, piece.shape[0], 128):
            unit, _ = normalize(piece[start : start + 128, :])
            unit_ref[base : base + 128, :] = unit.astype(jnp.bfloat16)
            base += 128


def attend(own, others, temper, offset, first_row=None):
    logits = (
        temper
        * lax.dot_general(own, others, (((1,), (1,)), ((), ())), preferred_element_type=jnp.float32)
        + offset
    )
    weights = jax.nn.sigmoid(logits)
    if first_row is not None:
        across = lax.broadcasted_iota(jnp.int32, logits.shape, 0) + first_row
        down = lax.broadcasted_iota(jnp.int32, logits.shape, 1)
        weights = weights - jnp.where(across == down, 1.0, 0.0)
    return jnp.dot(weights.astype(jnp.bfloat16), others, preferred_element_type=jnp.float32)


def piece_kernel(inner, first, img_ref, txt_ref, *refs):
    *_, out_ref, sem = refs

    def fetch(raw_ref):
        copy = pltpu.make_async_copy(raw_ref.at[pl.ds(first, out_ref.shape[0]), :], out_ref, sem)
        copy.start()
        copy.wait()

    inner_ref, outer_ref = functools.partial(fetch, txt_ref), functools.partial(fetch, img_ref)
    on_even(inner_ref, outer_ref) if inner else on_even(outer_ref, inner_ref)


def gate_kernel(*refs):
    del refs


def own_kernel(temper_ref, offset_ref, img_ref, txt_ref, *outs):
    raws, sums, units, inverses = outs[:2], outs[2:4], outs[4:6], outs[6:]
    temper, offset = temper_ref[0], offset_ref[0]

    def take(*sources):
        for source, raw in zip(sources, raws):
            raw[...] = source[...]

    on_even(lambda: take(txt_ref, img_ref), lambda: take(img_ref, txt_ref))
    for raw, unit_ref, inverse_ref in zip(raws, units, inverses):

        @pl.loop(0, raw.shape[0] // 128)
        def _(i, raw=raw, unit_ref=unit_ref, inverse_ref=inverse_ref):
            rows = pl.ds(pl.multiple_of(i * 128, 128), 128)
            unit, inverse = normalize(raw[rows, :])
            unit_ref[rows, :] = unit.astype(jnp.bfloat16)
            inverse_ref[rows, :] = jnp.broadcast_to(inverse, (128, lanes))

    @pl.loop(0, img_ref.shape[0] // tile)
    def _(i):
        first = pl.multiple_of(i * tile, tile)
        rows = pl.ds(first, tile)
        for side in range(2):
            sums[side][rows, :] = attend(
                units[side][rows, :], units[1 - side][...], temper, offset, first
            )


def more_kernel(pieces, onward, temper_ref, offset_ref, own_unit, sum_ref, *refs):
    piece_refs, (out_ref, *onward_refs, others) = refs[:pieces], refs[pieces:]
    temper, offset = temper_ref[0], offset_ref[0]
    unit_rows(piece_refs, others)
    if onward:
        onward_refs[0][...] = piece_refs[-1][...]
    for first in range(0, own_unit.shape[0], tile):
        rows = pl.ds(first, tile)
        out_ref[rows, :] = sum_ref[rows, :] + attend(
            own_unit[rows, :], others[...], temper, offset
        )


def last_kernel(inner, temper_ref, offset_ref, own_unit, sum_ref, raw_ref, inverse_ref, *refs):
    piece, *refs = refs if inner else (refs[0], *refs[3:])
    grad_img, grad_txt, others, ready, sems = refs
    temper, offset = temper_ref[0], offset_ref[0]
    unit_rows([piece], others)

    def copies(into, first):
        rows = pl.ds(first, tile)
        return pltpu.make_async_copy(ready.at[rows, :], into.at[rows, :], sems.at[first // tile])

    def on_target(do):
        into_txt, into_img = functools.partial(do, grad_txt), functools.partial(do, grad_img)
        on_even(into_txt, into_img) if inner else on_even(into_img, into_txt)

    for first in range(0, own_unit.shape[0], tile):
        rows = pl.ds(first, tile)
        total = sum_ref[rows, :] + attend(own_unit[rows, :], others[...], temper, offset)
        raw = raw_ref[rows, :].astype(jnp.float32)
        inverse = inverse_ref[rows, :1]
        scale = temper * inverse
        along = jnp.sum(raw * total, axis=1, keepdims=True)
        ready[rows, :] = scale * total - (scale * inverse * inverse * along) * raw
        on_target(lambda into, first=first: copies(into, first).start())

    def finish(into):
        for first in range(0, own_unit.shape[0], tile):
            copies(into, first).wait()

    on_target(finish)


scalar = pl.BlockSpec(memory_space=pltpu.SMEM)
on_chip = pl.BlockSpec(memory_space=pltpu.VMEM)
off_chip = pl.BlockSpec(memory_space=pltpu.HBM)
anywhere = pl.BlockSpec(memory_space=pl.ANY)


def pinned(*values):
    return [pltpu.with_memory_space_constraint(value, pltpu.VMEM) for value in values]


def limit(mebibytes):
    return pltpu.CompilerParams(vmem_limit_bytes=mebibytes * 2**20)


def costs(rows, others, width, weight):
    return pl.CostEstimate(
        flops=int(weight * rows * others * width),
        bytes_accessed=4 * rows * width,
        transcendentals=0,
    )


small = pl.CostEstimate(flops=0, bytes_accessed=2**10, transcendentals=0)


def piece_of(images, texts, inner, first, last, tokens):
    raws = [images, texts]
    if not tokens:
        raws = [pltpu.with_memory_space_constraint(raw, pltpu.HBM) for raw in raws]
    return pl.pallas_call(
        functools.partial(piece_kernel, inner, first),
        in_specs=[anywhere if tokens else off_chip] * 2 + [anywhere] * len(tokens),
        out_specs=on_chip,
        out_shape=pltpu.VMEM((last - first, images.shape[1]), images.dtype),
        scratch_shapes=[pltpu.SemaphoreType.DMA],
        compiler_params=limit(1),
        cost_estimate=small,
    )(*raws, *tokens)


def gate(token, *values):
    count = len(values)
    return pl.pallas_call(
        gate_kernel,
        in_specs=[anywhere] + [on_chip] * count,
        out_specs=[on_chip] * count,
        out_shape=[pltpu.VMEM(value.shape, value.dtype) for value in values],
        input_output_aliases={1 + i: i for i in range(count)},
        compiler_params=limit(1),
        cost_estimate=small,
    )(token, *pinned(*values))


def own_block(temper, offset, images, texts):
    rows, width = images.shape
    raws = pltpu.VMEM((rows, width), jnp.bfloat16)
    sums = pltpu.VMEM((rows, width), jnp.float32)
    inverses = pltpu.VMEM((rows, lanes), jnp.float32)
    return pl.pallas_call(
        own_kernel,
        in_specs=[scalar] * 2 + [on_chip] * 2,
        out_specs=[on_chip] * 8,
        out_shape=[raws, raws, sums, sums, raws, raws, inverses, inverses],
        compiler_params=limit(16),
        cost_estimate=costs(rows, rows, width, 32),
    )(temper, offset, *pinned(images, texts))


def more_block(temper, offset, unit, sums, pieces, onward, weight):
    rows, width = unit.shape
    others = sum(piece.shape[0] for piece in pieces)
    return pl.pallas_call(
        functools.partial(more_kernel, len(pieces), onward),
        in_specs=[scalar] * 2 + [on_chip] * (2 + len(pieces)),
        out_specs=[on_chip] * (1 + onward),
        out_shape=[pltpu.VMEM((rows, width), jnp.float32)]
        + [pltpu.VMEM(pieces[-1].shape, jnp.bfloat16)] * onward,
        input_output_aliases={3: 0},
        scratch_shapes=[pltpu.VMEM((others, width), jnp.bfloat16)],
        compiler_params=limit(16),
        cost_estimate=costs(rows, others, width, weight),
    )(temper, offset, *pinned(unit, sums, *pieces))


def last_block(temper, offset, unit, sums, raw, inverse, piece, grads):
    rows, width = unit.shape
    inner = not grads
    return pl.pallas_call(
        functools.partial(last_kernel, inner),
        in_specs=[scalar] * 2 + [on_chip] * 5 + [off_chip] * len(grads),
        out_specs=[off_chip] * 2,
        out_shape=[jax.ShapeDtypeStruct((rows, width), jnp.float32)] * 2,
        input_output_aliases={} if inner else {7: 0, 8: 1},
        scratch_shapes=[
            pltpu.VMEM(piece.shape, jnp.bfloat16),
            pltpu.VMEM((rows, width), jnp.float32),
            pltpu.SemaphoreType.DMA((rows // tile,)),
        ],
        compiler_params=limit(16),
        cost_estimate=costs(rows, piece.shape[0], width, 16),
    )(temper, offset, *pinned(unit, sums, raw, inverse, piece), *grads)


def local(images, texts, log_scale, logit_bias):
    temper = jnp.exp(log_scale)
    rows = images.shape[0]
    near_inner, near_outer = [], []
    tokens = []
    for part in ((0, split), (split, rows)):
        for inner, near in ((True, near_inner), (False, near_outer)):
            piece = piece_of(images, texts, inner, *part, tokens)
            near.append(exchanged(piece, inner))
            tokens = [piece]
    raw_inner, raw_outer, sum_inner, sum_outer, unit_inner, unit_outer, inv_inner, inv_outer = (
        own_block(temper, logit_bias, images, texts)
    )
    near_inner[0], near_outer[0] = gate(inv_inner, near_inner[0], near_outer[0])
    far_outer = exchanged(near_inner[0], False)
    far_inner = exchanged(near_outer[0], True)
    more = functools.partial(more_block, temper, logit_bias)
    near_inner[1], near_outer[1] = gate(inv_inner, near_inner[1], near_outer[1])
    sum_inner, on_inner = more(unit_inner, sum_inner, near_inner, 1, 12)
    sum_outer, on_outer = more(unit_outer, sum_outer, near_outer, 1, 0.01)
    last_outer = exchanged(on_inner, False)
    last_inner = exchanged(on_outer, True)
    (sum_inner,) = more(unit_inner, sum_inner, [far_inner], 0, 0.01)
    (far_outer,) = gate(sum_inner, far_outer)
    (sum_outer,) = more(unit_outer, sum_outer, [far_outer], 0, 0.01)
    (last_inner,) = gate(sum_outer, last_inner)
    last = functools.partial(last_block, temper, logit_bias)
    grads = last(unit_inner, sum_inner, raw_inner, inv_inner, last_inner, ())
    return tuple(last(unit_outer, sum_outer, raw_outer, inv_outer, last_outer, grads))


def solution(mesh):
    return jax.shard_map(
        local,
        mesh=mesh,
        in_specs=(P(axes, None), P(axes, None), P(), P()),
        out_specs=(P(axes, None), P(axes, None)),
        check_vma=False,
    )
```

time: 345 us -> 118 us (0.34)
  the two profiles are of different devices: /device:TPU:16 before, /device:TPU:0 now
where the time goes in v2:
time: 118 us
  Pallas kernels  50.7 us (43%)
  waiting for transfers between devices  39.8 us (34%)
  starting transfers between devices  25.4 us (22%)
  between operations  2.26 us (2%)
    ppermute x8, waiting for transfers between devices, exchanged(): return lax.ppermute(value, axes, pairs)  39.8 us
    ppermute x8, starting transfers between devices, exchanged(): return lax.ppermute(value, axes, pairs)  25.4 us
    pallas_call x4, Pallas kernels, more_block(): pl.pallas_call(functools.partial(more_kernel, len(pieces), onward), in_sp...  25 us
    pallas_call x1, Pallas kernels, own_block(): pl.pallas_call(own_kernel, in_specs=[scalar] * 2 + [on_chip] * 2, out_spe...  14.8 us
    pallas_call x2, Pallas kernels, last_block(): pl.pallas_call(functools.partial(last_kernel, inner), in_specs=[scalar] *...  8.59 us
  transfers between devices with their start and end apart: 8, of which 5 were waited for; matrix products, arithmetic and copies ran while one was open for 0% of the time, Pallas kernels for 38%

profile of v2, /device:TPU:0, one launch (start us, length us, event | category | flops | bytes accessed | tf_op | source)
XLA Modules:
  0.0 118.2 jit_solution(13060611457821806481)
XLA Ops:
  0.6 0.0 copy-start.1
  0.6 0.0 copy-start
  0.6 1.6 %shard_map.60.refs_0_ = bf16[768,1152]{1,0:T(8,128)(2,1)S(1)} custom-call(bf16[1024,1152]{1,0:T(8,128)(2,1)} %img_ref.9, bf16[1024,1152]{1,0:T(8,128)(2,1)} %txt_ref.9), custom_call_target="tpu_custom_call" | custom-call | bytes 1024 | tf_op jit(solution)/shard_map/pallas_call | solution.py:180
  2.3 1.7 %collective-permute-start = (bf16[768,1152]{1,0:T(8,128)(2,1)S(1)}, bf16[768,1152]{1,0:T(8,128)(2,1)S(1)}, u32[]{:S(2)}, u32[]{:S(2)}) collective-permute-start(bf16[768,1152]{1,0:T(8,128)(2,1)S(1)} %shard_map.60.refs_0_), channel_id=1, source_target_pairs={{0,1},{1,0},{2,3},{3,2},{4,5},{5,4},{6,7},{7,6},{8,9},{9,8},{10,11... | collective-permute-start | bytes 5308424 | tf_op jit(solution)/shard_map/ppermute | solution.py:25
  4.0 0.0 copy-done.1
  4.0 0.0 copy-done
  4.0 0.4 shard_map.61.refs_0_
  4.4 7.8 %collective-permute-start.1 = (bf16[768,1152]{1,0:T(8,128)(2,1)S(1)}, bf16[768,1152]{1,0:T(8,128)(2,1)S(1)}, u32[]{:S(2)}, u32[]{:S(2)}) collective-permute-start(bf16[768,1152]{1,0:T(8,128)(2,1)S(1)} %shard_map.61.refs_0_), channel_id=1, source_target_pairs={{1,2},{2,1},{3,4},{4,3},{5,6},{6,5},{7,8},{8,7},{9,10},{10,9},{11,... | collective-permute-start | bytes 5308424 | tf_op jit(solution)/shard_map/ppermute | solution.py:25
  12.2 0.1 shard_map.63.refs_0_
  12.3 0.1 collective-permute-start.2
  12.4 0.1 shard_map.64
  12.6 0.7 collective-permute-start.3
  14.6 14.8 %shard_map.59 = (bf16[1024,1152]{1,0:T(8,128)(2,1)S(1)}, bf16[1024,1152]{1,0:T(8,128)(2,1)S(1)}, f32[1024,1152]{1,0:T(8,128)S(1)}, f32[1024,1152]{1,0:T(8,128)S(...) custom-call(f32[1]{0:T(128)S(6)} %exp.3.temper_ref, ...), custom_call_target="tpu_custom_call" | custom-call | flops 38654705664 | bytes 4718592 | tf_op jit(solution)/shard_map/pallas_call | solution.py:209
  29.4 21.8 %collective-permute-done.1.refs_2_ = bf16[768,1152]{1,0:T(8,128)(2,1)S(1)} collective-permute-done((bf16[768,1152]{1,0:T(8,128)(2,1)S(1)}, bf16[768,1152]{1,0:T(8,128)(2,1)S(1)}, u32[]{:S(2)}, u32[]{:S(2)}) %collective-permute-start.1) | collective-permute-done | bytes 1769504 | tf_op jit(solution)/shard_map/ppermute | solution.py:25
  51.3 0.0 collective-permute-done.refs_1_
  51.3 0.0 collective-permute-start.4
  51.3 7.4 %collective-permute-start.5 = (bf16[768,1152]{1,0:T(8,128)(2,1)S(1)}, bf16[768,1152]{1,0:T(8,128)(2,1)S(1)}, u32[]{:S(2)}, u32[]{:S(2)}) collective-permute-start(bf16[768,1152]{1,0:T(8,128)(2,1)S(1)} %get-tuple-element.28.refs_0_), channel_id=1, source_target_pairs={{1,2},{2,1},{3,4},{4,3},{5,6},{6,5},{7,8},{8,7},{9,10},{10,9},{11,... | collective-permute-start | bytes 5308424 | tf_op jit(solution)/shard_map/ppermute | solution.py:25
  58.7 5.2 %collective-permute-done.3.refs_2_ = bf16[256,1152]{1,0:T(8,128)(2,1)S(1)} collective-permute-done((bf16[256,1152]{1,0:T(8,128)(2,1)S(1)}, bf16[256,1152]{1,0:T(8,128)(2,1)S(1)}, u32[]{:S(2)}, u32[]{:S(2)}) %collective-permute-start.3) | collective-permute-done | bytes 589856 | tf_op jit(solution)/shard_map/ppermute | solution.py:25
  63.9 0.0 collective-permute-done.2.refs_1_
  63.9 7.3 %shard_map.66 = (f32[1024,1152]{1,0:T(8,128)S(1)}, bf16[256,1152]{1,0:T(8,128)(2,1)S(1)}) custom-call(f32[1]{0:T(128)S(6)} %exp.3.temper_ref, f32[1]{0:T(128)S(6)} %copy.31.offset_ref, bf16[1024,1152]{1,0:T(8,128)(2,1)S(1)} %get-tuple-element.20.own_unit, f32[1024,1152]{1,0:T(8,128)S(1)} %get-tuple-element.21.sum_ref, ...), custom_call_target="tpu_custom_call", output_to_operand_aliasing={{0}: (3, {})} | custom-call | flops 12079595 | bytes 4718592 | tf_op jit(solution)/shard_map/pallas_call | solution.py:222
  71.3 0.3 collective-permute-start.7
  71.5 7.3 %shard_map.67 = (f32[1024,1152]{1,0:T(8,128)S(1)}, bf16[256,1152]{1,0:T(8,128)(2,1)S(1)}) custom-call(f32[1]{0:T(128)S(6)} %exp.3.temper_ref, f32[1]{0:T(128)S(6)} %copy.31.offset_ref, bf16[1024,1152]{1,0:T(8,128)(2,1)S(1)} %get-tuple-element.26.own_unit, f32[1024,1152]{1,0:T(8,128)S(1)} %get-tuple-element.27.sum_ref, ...), custom_call_target="tpu_custom_call", output_to_operand_aliasing={{0}: (3, {})} | custom-call | flops 14495514624 | bytes 4718592 | tf_op jit(solution)/shard_map/pallas_call | solution.py:222
  78.9 7.4 %collective-permute-start.6 = (bf16[256,1152]{1,0:T(8,128)(2,1)S(1)}, bf16[256,1152]{1,0:T(8,128)(2,1)S(1)}, u32[]{:S(2)}, u32[]{:S(2)}) collective-permute-start(bf16[256,1152]{1,0:T(8,128)(2,1)S(1)} %get-tuple-element.33), channel_id=1, source_target_pairs={{1,2},{2,1},{3,4},{4,3},{5,6},{6,5},{7,8},{8,7},{9,10},{10,9},{11,... | collective-permute-start | bytes 1769480 | tf_op jit(solution)/shard_map/ppermute | solution.py:25
  86.3 8.2 %collective-permute-done.4.refs_0_ = bf16[768,1152]{1,0:T(8,128)(2,1)S(1)} collective-permute-done((bf16[768,1152]{1,0:T(8,128)(2,1)S(1)}, bf16[768,1152]{1,0:T(8,128)(2,1)S(1)}, u32[]{:S(2)}, u32[]{:S(2)}) %collective-permute-start.4) | collective-permute-done | bytes 1769504 | tf_op jit(solution)/shard_map/ppermute | solution.py:25
  94.5 5.2 %shard_map.68.refs_0_.sum_ref = f32[1024,1152]{1,0:T(8,128)S(1)} custom-call(f32[1]{0:T(128)S(6)} %exp.3.temper_ref, f32[1]{0:T(128)S(6)} %copy.31.offset_ref, bf16[1024,1152]{1,0:T(8,128)(2,1)S(1)} %get-tuple-element.26.own_unit, f32[1024,1152]{1,0:T(8,128)S(1)} %get-tuple-element.30.sum_ref, ...), custom_call_target="tpu_custom_call", output_to_operand_aliasing={{}: (3, {})} | custom-call | flops 9059696 | bytes 4718592 | tf_op jit(solution)/shard_map/pallas_call | solution.py:222
  99.6 2.2 %collective-permute-done.5.refs_1_ = bf16[768,1152]{1,0:T(8,128)(2,1)S(1)} collective-permute-done((bf16[768,1152]{1,0:T(8,128)(2,1)S(1)}, bf16[768,1152]{1,0:T(8,128)(2,1)S(1)}, u32[]{:S(2)}, u32[]{:S(2)}) %collective-permute-start.5) | collective-permute-done | bytes 1769504 | tf_op jit(solution)/shard_map/ppermute | solution.py:25
  101.8 5.2 %shard_map.70.refs_0_.sum_ref = f32[1024,1152]{1,0:T(8,128)S(1)} custom-call(f32[1]{0:T(128)S(6)} %exp.3.temper_ref, f32[1]{0:T(128)S(6)} %copy.31.offset_ref, bf16[1024,1152]{1,0:T(8,128)(2,1)S(1)} %get-tuple-element.20.own_unit, f32[1024,1152]{1,0:T(8,128)S(1)} %get-tuple-element.25.sum_ref, ...), custom_call_target="tpu_custom_call", output_to_operand_aliasing={{}: (3, {})} | custom-call | flops 9059696 | bytes 4718592 | tf_op jit(solution)/shard_map/pallas_call | solution.py:222
  107.0 0.0 collective-permute-done.7.refs_1_
  107.0 4.3 %shard_map.72 = (f32[1024,1152]{1,0:T(8,128)}, f32[1024,1152]{1,0:T(8,128)}) custom-call(f32[1]{0:T(128)S(6)} %exp.3.temper_ref, f32[1]{0:T(128)S(6)} %copy.31.offset_ref, bf16[1024,1152]{1,0:T(8,128)(2,1)S(1)} %get-tuple-element.26.own_unit, f32[1024,1152]{1,0:T(8,128)S(1)} %shard_map.68.refs_0_.sum_ref, bf16[1024,1152]{1,0:T(8,128)(2,1)S(1)} %get-tuple-element.34.raw_ref, ...), custom_call_target="tpu_custom_call" | custom-call | flops 4831838208 | bytes 4718592 | tf_op jit(solution)/shard_map/pallas_call | solution.py:238
  111.3 2.4 %collective-permute-done.6.refs_0_ = bf16[256,1152]{1,0:T(8,128)(2,1)S(1)} collective-permute-done((bf16[256,1152]{1,0:T(8,128)(2,1)S(1)}, bf16[256,1152]{1,0:T(8,128)(2,1)S(1)}, u32[]{:S(2)}, u32[]{:S(2)}) %collective-permute-start.6) | collective-permute-done | bytes 589856 | tf_op jit(solution)/shard_map/ppermute | solution.py:25
  113.7 4.3 %shard_map.73 = (f32[1024,1152]{1,0:T(8,128)}, f32[1024,1152]{1,0:T(8,128)}) custom-call(f32[1]{0:T(128)S(6)} %exp.3.temper_ref, f32[1]{0:T(128)S(6)} %copy.31.offset_ref, bf16[1024,1152]{1,0:T(8,128)(2,1)S(1)} %get-tuple-element.20.own_unit, f32[1024,1152]{1,0:T(8,128)S(1)} %shard_map.70.refs_0_.sum_ref, ...), custom_call_target="tpu_custom_call", output_to_operand_aliasing={{0}: (7, {}), {1}: (8, {})} | custom-call | flops 4831838208 | bytes 4718592 | tf_op jit(solution)/shard_map/pallas_call | solution.py:238
  (4 shorter events, 0.0 us)
Async XLA Ops:
  0.6 3.4 %copy-start.1 = (bf16[1024,1152]{1,0:T(8,128)(2,1)S(1)}, bf16[1024,1152]{1,0:T(8,128)(2,1)}, u32[]{:S(2)}) copy-start(bf16[1024,1152]{1,0:T(8,128)(2,1)} %txt_ref.9) | copy-start | bytes 7077892
  0.6 3.4 %copy-start = (bf16[1024,1152]{1,0:T(8,128)(2,1)S(1)}, bf16[1024,1152]{1,0:T(8,128)(2,1)}, u32[]{:S(2)}) copy-start(bf16[1024,1152]{1,0:T(8,128)(2,1)} %img_ref.9) | copy-start | bytes 7077892
  2.3 49.0 %collective-permute-start = (bf16[768,1152]{1,0:T(8,128)(2,1)S(1)}, bf16[768,1152]{1,0:T(8,128)(2,1)S(1)}, u32[]{:S(2)}, u32[]{:S(2)}) collective-permute-start(bf16[768,1152]{1,0:T(8,128)(2,1)S(1)} %shard_map.60.refs_0_), channel_id=1, source_target_pairs={{0,1},{1,0},{2,3},{3,2},{4,5},{5,4},{6,7},{7,6},{8,9},{9,8},{10,11... | collective-permute-start | bytes 5308424 | tf_op jit(solution)/shard_map/ppermute | solution.py:25
  4.4 46.8 %collective-permute-start.1 = (bf16[768,1152]{1,0:T(8,128)(2,1)S(1)}, bf16[768,1152]{1,0:T(8,128)(2,1)S(1)}, u32[]{:S(2)}, u32[]{:S(2)}) collective-permute-start(bf16[768,1152]{1,0:T(8,128)(2,1)S(1)} %shard_map.61.refs_0_), channel_id=1, source_target_pairs={{1,2},{2,1},{3,4},{4,3},{5,6},{6,5},{7,8},{8,7},{9,10},{10,9},{11,... | collective-permute-start | bytes 5308424 | tf_op jit(solution)/shard_map/ppermute | solution.py:25
  12.3 51.6 %collective-permute-start.2 = (bf16[256,1152]{1,0:T(8,128)(2,1)S(1)}, bf16[256,1152]{1,0:T(8,128)(2,1)S(1)}, u32[]{:S(2)}, u32[]{:S(2)}) collective-permute-start(bf16[256,1152]{1,0:T(8,128)(2,1)S(1)} %shard_map.63.refs_0_), channel_id=1, source_target_pairs={{0,1},{1,0},{2,3},{3,2},{4,5},{5,4},{6,7},{7,6},{8,9},{9,8},{10,11... | collective-permute-start | bytes 1769480 | tf_op jit(solution)/shard_map/ppermute | solution.py:25
  12.6 51.3 %collective-permute-start.3 = (bf16[256,1152]{1,0:T(8,128)(2,1)S(1)}, bf16[256,1152]{1,0:T(8,128)(2,1)S(1)}, u32[]{:S(2)}, u32[]{:S(2)}) collective-permute-start(bf16[256,1152]{1,0:T(8,128)(2,1)S(1)} %shard_map.64), channel_id=1, source_target_pairs={{1,2},{2,1},{3,4},{4,3},{5,6},{6,5},{7,8},{8,7},{9,10},{10,9},{11,... | collective-permute-start | bytes 1769480 | tf_op jit(solution)/shard_map/ppermute | solution.py:25
  51.3 43.2 %collective-permute-start.4 = (bf16[768,1152]{1,0:T(8,128)(2,1)S(1)}, bf16[768,1152]{1,0:T(8,128)(2,1)S(1)}, u32[]{:S(2)}, u32[]{:S(2)}) collective-permute-start(bf16[768,1152]{1,0:T(8,128)(2,1)S(1)} %get-tuple-element.23.refs_0_), channel_id=1, source_target_pairs={{0,1},{1,0},{2,3},{3,2},{4,5},{5,4},{6,7},{7,6},{8,9},{9,8},{10,11... | collective-permute-start | bytes 5308424 | tf_op jit(solution)/shard_map/ppermute | solution.py:25
  51.3 50.6 %collective-permute-start.5 = (bf16[768,1152]{1,0:T(8,128)(2,1)S(1)}, bf16[768,1152]{1,0:T(8,128)(2,1)S(1)}, u32[]{:S(2)}, u32[]{:S(2)}) collective-permute-start(bf16[768,1152]{1,0:T(8,128)(2,1)S(1)} %get-tuple-element.28.refs_0_), channel_id=1, source_target_pairs={{1,2},{2,1},{3,4},{4,3},{5,6},{6,5},{7,8},{8,7},{9,10},{10,9},{11,... | collective-permute-start | bytes 5308424 | tf_op jit(solution)/shard_map/ppermute | solution.py:25
  71.3 35.8 %collective-permute-start.7 = (bf16[256,1152]{1,0:T(8,128)(2,1)S(1)}, bf16[256,1152]{1,0:T(8,128)(2,1)S(1)}, u32[]{:S(2)}, u32[]{:S(2)}) collective-permute-start(bf16[256,1152]{1,0:T(8,128)(2,1)S(1)} %get-tuple-element.35), channel_id=1, source_target_pairs={{0,1},{1,0},{2,3},{3,2},{4,5},{5,4},{6,7},{7,6},{8,9},{9,8},{10,11... | collective-permute-start | bytes 1769480 | tf_op jit(solution)/shard_map/ppermute | solution.py:25
  78.9 34.9 %collective-permute-start.6 = (bf16[256,1152]{1,0:T(8,128)(2,1)S(1)}, bf16[256,1152]{1,0:T(8,128)(2,1)S(1)}, u32[]{:S(2)}, u32[]{:S(2)}) collective-permute-start(bf16[256,1152]{1,0:T(8,128)(2,1)S(1)} %get-tuple-element.33), channel_id=1, source_target_pairs={{1,2},{2,1},{3,4},{4,3},{5,6},{6,5},{7,8},{8,7},{9,10},{10,9},{11,... | collective-permute-start | bytes 1769480 | tf_op jit(solution)/shard_map/ppermute | solution.py:25

commit v3 on v2

v3 whole, which is shorter than its diff:
```python
import functools

import jax
import jax.numpy as jnp
from jax import lax
from jax.experimental import pallas as pl
from jax.experimental.pallas import tpu as pltpu
from jax.sharding import PartitionSpec as P


epsilon = 1e-06
axes = ("grp", "dev")
start = 256
split = 768
tile = 256
lanes = 128


def exchanged(value, inner):
    count = lax.axis_size(axes)
    first = 0 if inner else 1
    pairs = []
    for low in range(first, count, 2):
        high = (low + 1) % count
        pairs += [(low, high), (high, low)]
    return lax.ppermute(value, axes, pairs)


def on_even(is_even, is_odd):
    odd = lax.rem(lax.axis_index("dev"), 2)
    pl.when(odd == 0)(is_even)
    pl.when(odd == 1)(is_odd)


def normalize(raw_rows):
    rows32 = raw_rows.astype(jnp.float32)
    inverse = lax.rsqrt(jnp.sum(rows32 * rows32, axis=1, keepdims=True) + epsilon)
    return rows32 * inverse, inverse


def unit_rows(piece, unit_ref, first=0, inverse_ref=None):
    @pl.loop(0, piece.shape[0] // 128)
    def _(i):
        rows = pl.ds(pl.multiple_of(i * 128, 128), 128)
        into = pl.ds(pl.multiple_of(first + i * 128, 128), 128)
        unit, inverse = normalize(piece[rows, :])
        unit_ref[into, :] = unit.astype(jnp.bfloat16)
        if inverse_ref is not None:
            inverse_ref[into, :] = jnp.broadcast_to(inverse, (128, lanes))


def weigh(own, others, temper, offset, first_row=None):
    logits = (
        temper
        * lax.dot_general(own, others, (((1,), (1,)), ((), ())), preferred_element_type=jnp.float32)
        + offset
    )
    weights = jax.nn.sigmoid(logits)
    if first_row is not None:
        across = lax.broadcasted_iota(jnp.int32, logits.shape, 0) + first_row
        down = lax.broadcasted_iota(jnp.int32, logits.shape, 1)
        weights = weights - jnp.where(across == down, 1.0, 0.0)
    return weights.astype(jnp.bfloat16)


def attend(own_unit, others, temper, offset, sum_ref, finish):
    tiles = [pl.ds(first, tile) for first in range(0, own_unit.shape[0], tile)]
    ahead = weigh(own_unit[tiles[0], :], others[...], temper, offset)
    for rows, following in zip(tiles, tiles[1:] + [None]):
        weights = ahead
        if following is not None:
            ahead = weigh(own_unit[following, :], others[...], temper, offset)
        finish(
            rows,
            sum_ref[rows, :] + jnp.dot(weights, others[...], preferred_element_type=jnp.float32),
        )


def pieces_kernel(first, img_ref, txt_ref, *refs):
    inner_ref, outer_ref, sems = refs[-3:]
    rows = pl.ds(first, inner_ref.shape[0])

    def fetch(*raws):
        copies = [
            pltpu.make_async_copy(raw.at[rows, :], out, sems.at[i])
            for i, (raw, out) in enumerate(zip(raws, (inner_ref, outer_ref)))
        ]
        for copy in copies:
            copy.start()
        for copy in copies:
            copy.wait()

    on_even(lambda: fetch(txt_ref, img_ref), lambda: fetch(img_ref, txt_ref))


def gate_kernel(*refs):
    del refs


def first_kernel(token_ref, inner_ref, outer_ref, inner_unit, outer_unit):
    unit_rows(inner_ref, inner_unit)
    unit_rows(outer_ref, outer_unit)


def rest_kernel(*refs):
    for first_unit, rest, whole, middle, last in (refs[0::2], refs[1::2]):
        count = first_unit.shape[0]
        whole[pl.ds(0, count), :] = first_unit[...]
        unit_rows(rest, whole, count)
        middle[...] = whole[pl.ds(count, middle.shape[0]), :]
        last[...] = whole[pl.ds(count + middle.shape[0], last.shape[0]), :]


def own_kernel(temper_ref, offset_ref, img_ref, txt_ref, *outs):
    raws, sums, units, inverses, sems = outs[:2], outs[2:4], outs[4:6], outs[6:8], outs[8]
    temper, offset = temper_ref[0], offset_ref[0]

    def fetch(*sources):
        copies = [
            pltpu.make_async_copy(source, raw, sems.at[i])
            for i, (source, raw) in enumerate(zip(sources, raws))
        ]
        for copy in copies:
            copy.start()
        for copy in copies:
            copy.wait()

    on_even(lambda: fetch(txt_ref, img_ref), lambda: fetch(img_ref, txt_ref))
    for raw, unit_ref, inverse_ref in zip(raws, units, inverses):
        unit_rows(raw, unit_ref, 0, inverse_ref)

    @pl.loop(0, img_ref.shape[0] // tile)
    def _(i):
        first = pl.multiple_of(i * tile, tile)
        rows = pl.ds(first, tile)
        for side in range(2):
            others = units[1 - side][...]
            weights = weigh(units[side][rows, :], others, temper, offset, first)
            sums[side][rows, :] = jnp.dot(weights, others, preferred_element_type=jnp.float32)


def near_kernel(temper_ref, offset_ref, own_unit, sum_ref, others, out_ref):
    def finish(rows, total):
        out_ref[rows, :] = total

    attend(own_unit, others, temper_ref[0], offset_ref[0], sum_ref, finish)


def far_kernel(temper_ref, offset_ref, own_unit, sum_ref, first, middle, out_ref, others):
    def finish(rows, total):
        out_ref[rows, :] = total

    count = first.shape[0]
    others[pl.ds(0, count), :] = first[...]
    others[pl.ds(count, middle.shape[0]), :] = middle[...]
    attend(own_unit, others, temper_ref[0], offset_ref[0], sum_ref, finish)


def last_kernel(inner, temper_ref, offset_ref, own_unit, sum_ref, raw_ref, inverse_ref, *refs):
    others, *refs = refs if inner else (refs[0], *refs[3:])
    grad_img, grad_txt, ready, sems = refs
    temper = temper_ref[0]

    def copies(into, rows):
        return pltpu.make_async_copy(
            ready.at[rows, :], into.at[rows, :], sems.at[rows.start // tile]
        )

    def on_target(do):
        into_txt, into_img = functools.partial(do, grad_txt), functools.partial(do, grad_img)
        on_even(into_txt, into_img) if inner else on_even(into_img, into_txt)

    def finish(rows, total):
        raw = raw_ref[rows, :].astype(jnp.float32)
        inverse = inverse_ref[rows, :1]
        scale = temper * inverse
        along = jnp.sum(raw * total, axis=1, keepdims=True)
        ready[rows, :] = scale * total - (scale * inverse * inverse * along) * raw
        on_target(lambda into: copies(into, rows).start())

    attend(own_unit, others, temper, offset_ref[0], sum_ref, finish)

    def wait(into):
        for first in range(0, own_unit.shape[0], tile):
            copies(into, pl.ds(first, tile)).wait()

    on_target(wait)


scalar = pl.BlockSpec(memory_space=pltpu.SMEM)
on_chip = pl.BlockSpec(memory_space=pltpu.VMEM)
off_chip = pl.BlockSpec(memory_space=pltpu.HBM)
anywhere = pl.BlockSpec(memory_space=pl.ANY)


def pinned(*values, memory=pltpu.VMEM):
    return [pltpu.with_memory_space_constraint(value, memory) for value in values]


def limit(mebibytes):
    return pltpu.CompilerParams(vmem_limit_bytes=mebibytes * 2**20)


def costs(rows, others, width, weight):
    return pl.CostEstimate(
        flops=int(weight * rows * others * width),
        bytes_accessed=4 * rows * width,
        transcendentals=0,
    )


small = pl.CostEstimate(flops=0, bytes_accessed=2**10, transcendentals=0)


def held(rows, like, dtype=jnp.bfloat16):
    return pltpu.VMEM((rows, like.shape[1]), dtype)


def pieces_of(images, texts, first, last, tokens):
    return pl.pallas_call(
        functools.partial(pieces_kernel, first),
        in_specs=[off_chip] * 2 + [anywhere] * len(tokens),
        out_specs=[on_chip] * 2,
        out_shape=[held(last - first, images)] * 2,
        scratch_shapes=[pltpu.SemaphoreType.DMA((2,))],
        compiler_params=limit(1),
        cost_estimate=small,
    )(*pinned(images, texts, memory=pltpu.HBM), *tokens)


def first_units(token, inner, outer):
    return pl.pallas_call(
        first_kernel,
        in_specs=[anywhere] + [on_chip] * 2,
        out_specs=[on_chip] * 2,
        out_shape=[held(inner.shape[0], inner)] * 2,
        compiler_params=limit(4),
        cost_estimate=small,
    )(token, *pinned(inner, outer))


def rest_units(firsts, rests):
    count, width = firsts[0].shape[0], firsts[0]
    more = rests[0].shape[0]
    sizes = (count + more, split - count, count + more - split)
    return pl.pallas_call(
        rest_kernel,
        in_specs=[on_chip] * 4,
        out_specs=[on_chip] * 6,
        out_shape=[held(size, width) for size in sizes for _ in range(2)],
        compiler_params=limit(4),
        cost_estimate=small,
    )(*pinned(*firsts, *rests))


def gate(token, *values):
    count = len(values)
    return pl.pallas_call(
        gate_kernel,
        in_specs=[anywhere] + [on_chip] * count,
        out_specs=[on_chip] * count,
        out_shape=[pltpu.VMEM(value.shape, value.dtype) for value in values],
        input_output_aliases={1 + i: i for i in range(count)},
        compiler_params=limit(1),
        cost_estimate=small,
    )(token, *pinned(*values))


def own_block(temper, offset, images, texts):
    rows = images.shape[0]
    raws, sums = held(rows, images), held(rows, images, jnp.float32)
    inverses = pltpu.VMEM((rows, lanes), jnp.float32)
    return pl.pallas_call(
        own_kernel,
        in_specs=[scalar] * 2 + [off_chip] * 2,
        out_specs=[on_chip] * 8,
        out_shape=[raws, raws, sums, sums, raws, raws, inverses, inverses],
        scratch_shapes=[pltpu.SemaphoreType.DMA((2,))],
        compiler_params=limit(16),
        cost_estimate=costs(rows, rows, images.shape[1], 32),
    )(temper, offset, *pinned(images, texts, memory=pltpu.HBM))


def more_block(temper, offset, unit, sums, pieces, weight):
    rows, width = unit.shape
    others = sum(piece.shape[0] for piece in pieces)
    several = len(pieces) > 1
    return pl.pallas_call(
        far_kernel if several else near_kernel,
        in_specs=[scalar] * 2 + [on_chip] * (2 + len(pieces)),
        out_specs=on_chip,
        out_shape=held(rows, unit, jnp.float32),
        input_output_aliases={3: 0},
        scratch_shapes=[pltpu.VMEM((others, width), jnp.bfloat16)] * several,
        compiler_params=limit(16),
        cost_estimate=costs(rows, others, width, weight),
    )(temper, offset, *pinned(unit, sums, *pieces))


def last_block(temper, offset, unit, sums, raw, inverse, piece, grads):
    rows, width = unit.shape
    inner = not grads
    return pl.pallas_call(
        functools.partial(last_kernel, inner),
        in_specs=[scalar] * 2 + [on_chip] * 5 + [off_chip] * len(grads),
        out_specs=[off_chip] * 2,
        out_shape=[jax.ShapeDtypeStruct((rows, width), jnp.float32)] * 2,
        input_output_aliases={} if inner else {7: 0, 8: 1},
        scratch_shapes=[
            pltpu.VMEM((rows, width), jnp.float32),
            pltpu.SemaphoreType.DMA((rows // tile,)),
        ],
        compiler_params=limit(16),
        cost_estimate=costs(rows, piece.shape[0], width, 16),
    )(temper, offset, *pinned(unit, sums, raw, inverse, piece), *grads)


def local(images, texts, log_scale, logit_bias):
    temper = jnp.exp(log_scale)
    rows = images.shape[0]
    pieces = pieces_of(images, texts, 0, start, [])
    pieces = [pieces[0], gate(pieces[0], pieces[1])[0]]
    firsts = [exchanged(pieces[0], True), exchanged(pieces[1], False)]
    pieces = pieces_of(images, texts, start, rows, pieces[:1])
    rests = [exchanged(pieces[0], True), exchanged(pieces[1], False)]
    raw_inner, raw_outer, sum_inner, sum_outer, unit_inner, unit_outer, inv_inner, inv_outer = (
        own_block(temper, logit_bias, images, texts)
    )
    firsts = first_units(inv_inner, *firsts)
    far_outer, far_inner = exchanged(firsts[0], False), exchanged(firsts[1], True)
    near_inner, near_outer, *middles, last_inner, last_outer = rest_units(firsts, rests)
    middle_outer, middle_inner = exchanged(middles[0], False), exchanged(middles[1], True)
    more = functools.partial(more_block, temper, logit_bias)
    sum_inner = more(unit_inner, sum_inner, [near_inner], 6)
    sum_outer = more(unit_outer, sum_outer, [near_outer], 6)
    last_inner, last_outer, far_inner, far_outer = gate(
        sum_outer, last_inner, last_outer, far_inner, far_outer
    )
    last_outer, last_inner = exchanged(last_inner, False), exchanged(last_outer, True)
    sum_inner = more(unit_inner, sum_inner, [far_inner, middle_inner], 0.01)
    (middle_outer,) = gate(sum_inner, middle_outer)
    sum_outer = more(unit_outer, sum_outer, [far_outer, middle_outer], 0.01)
    (last_inner,) = gate(sum_outer, last_inner)
    last = functools.partial(last_block, temper, logit_bias)
    grads = last(unit_inner, sum_inner, raw_inner, inv_inner, last_inner, ())
    return tuple(last(unit_outer, sum_outer, raw_outer, inv_outer, last_outer, grads))


def solution(mesh):
    return jax.shard_map(
        local,
        mesh=mesh,
        in_specs=(P(axes, None), P(axes, None), P(), P()),
        out_specs=(P(axes, None), P(axes, None)),
        check_vma=False,
    )
```

time: 118 us -> 117 us (level)
  waiting for transfers between devices: 39.8 us -> 33.8 us
  starting transfers between devices: 25.4 us -> 28.1 us
  Pallas kernels: 50.7 us -> 52.2 us
    ppermute x8 -> x10, waiting for transfers between devices: 39.8 us -> 33.8 us  [exchanged(): return lax.ppermute(value, axes, pairs)]
    ppermute x8 -> x10, starting transfers between devices: 25.4 us -> 28.1 us  [exchanged(): return lax.ppermute(value, axes, pairs)]
    pallas_call x9, Pallas kernels: 42.1 us -> 44.1 us  [the longest x4 21.2 us: more_block(): pl.pallas_call(far_kernel if several else near_kernel, in_specs=[scalar]...]
  transfers between devices with their start and end apart: 8 -> 10, of which waited for: 5 -> 6; matrix products, arithmetic and copies ran while one was open for 0% -> 0% of each run, Pallas kernels for 38% -> 40%
where the time goes in v3:
time: 117 us; the launch traced here: 116 us
  Pallas kernels  52.2 us (45%)
  waiting for transfers between devices  33.8 us (29%)
  starting transfers between devices  28.1 us (24%)
  between operations  2.27 us (2%)
    ppermute x10, waiting for transfers between devices, exchanged(): return lax.ppermute(value, axes, pairs)  33.8 us
    ppermute x10, starting transfers between devices, exchanged(): return lax.ppermute(value, axes, pairs)  28.1 us
    pallas_call x4, Pallas kernels, more_block(): pl.pallas_call(far_kernel if several else near_kernel, in_specs=[scalar]...  21.2 us
    pallas_call x1, Pallas kernels, own_block(): pl.pallas_call(own_kernel, in_specs=[scalar] * 2 + [off_chip] * 2, out_sp...  16.9 us
    pallas_call x2, Pallas kernels, last_block(): pl.pallas_call(functools.partial(last_kernel, inner), in_specs=[scalar] *...  8.12 us
    pallas_call x2, Pallas kernels, pieces_of(): pl.pallas_call(functools.partial(pieces_kernel, first), in_specs=[off_chi...  3.3 us
  transfers between devices with their start and end apart: 10, of which 6 were waited for; matrix products, arithmetic and copies ran while one was open for 0% of the time, Pallas kernels for 40%

profile of v3, /device:TPU:0, one launch (start us, length us, event | category | flops | bytes accessed | tf_op | source)
XLA Modules:
  0.0 116.3 jit_solution(17848970428811038691)
XLA Ops:
  0.6 1.3 %shard_map.60 = (bf16[256,1152]{1,0:T(8,128)(2,1)S(1)}, bf16[256,1152]{1,0:T(8,128)(2,1)S(1)}) custom-call(bf16[1024,1152]{1,0:T(8,128)(2,1)} %img_ref.5, bf16[1024,1152]{1,0:T(8,128)(2,1)} %txt_ref.5), custom_call_target="tpu_custom_call" | custom-call | bytes 1024 | tf_op jit(solution)/shard_map/pallas_call | solution.py:220
  1.9 1.7 %collective-permute-start = (bf16[256,1152]{1,0:T(8,128)(2,1)S(1)}, bf16[256,1152]{1,0:T(8,128)(2,1)S(1)}, u32[]{:S(2)}, u32[]{:S(2)}) collective-permute-start(bf16[256,1152]{1,0:T(8,128)(2,1)S(1)} %get-tuple-element.31.refs_0_), channel_id=1, source_target_pairs={{0,1},{1,0},{2,3},{3,2},{4,5},{5,4},{6,7},{7,6},{8,9},{9,8},{10,11... | collective-permute-start | bytes 1769480 | tf_op jit(solution)/shard_map/ppermute | solution.py:26
  3.7 7.0 %collective-permute-start.1 = (bf16[256,1152]{1,0:T(8,128)(2,1)S(1)}, bf16[256,1152]{1,0:T(8,128)(2,1)S(1)}, u32[]{:S(2)}, u32[]{:S(2)}) collective-permute-start(bf16[256,1152]{1,0:T(8,128)(2,1)S(1)} %shard_map.61), channel_id=1, source_target_pairs={{1,2},{2,1},{3,4},{4,3},{5,6},{6,5},{7,8},{8,7},{9,10},{10,9},{11,... | collective-permute-start | bytes 1769480 | tf_op jit(solution)/shard_map/ppermute | solution.py:26
  10.7 2.0 %shard_map.63 = (bf16[768,1152]{1,0:T(8,128)(2,1)S(1)}, bf16[768,1152]{1,0:T(8,128)(2,1)S(1)}) custom-call(bf16[1024,1152]{1,0:T(8,128)(2,1)} %img_ref.5, bf16[1024,1152]{1,0:T(8,128)(2,1)} %txt_ref.5, bf16[256,1152]{1,0:T(8,128)(2,1)S(1)} %get-tuple-element.31.refs_0_), custom_call_target="tpu_custom_call" | custom-call | bytes 1024 | tf_op jit(solution)/shard_map/pallas_call | solution.py:220
  12.7 0.1 collective-permute-start.2
  12.8 1.0 collective-permute-start.3
  15.1 16.9 %shard_map.59 = (bf16[1024,1152]{1,0:T(8,128)(2,1)S(1)}, bf16[1024,1152]{1,0:T(8,128)(2,1)S(1)}, f32[1024,1152]{1,0:T(8,128)S(1)}, f32[1024,1152]{1,0:T(8,128)S(...) custom-call(f32[1]{0:T(128)S(6)} %exp.3.temper_ref, ...), custom_call_target="tpu_custom_call" | custom-call | flops 38654705664 | bytes 4718592 | tf_op jit(solution)/shard_map/pallas_call | solution.py:273
  32.0 0.0 collective-permute-done.1.outer_ref
  32.0 0.0 collective-permute-done.inner_ref
  32.0 0.6 shard_map.62
  32.6 6.3 %collective-permute-start.5 = (bf16[256,1152]{1,0:T(8,128)(2,1)S(1)}, bf16[256,1152]{1,0:T(8,128)(2,1)S(1)}, u32[]{:S(2)}, u32[]{:S(2)}) collective-permute-start(bf16[256,1152]{1,0:T(8,128)(2,1)S(1)} %get-tuple-element.33.refs_0_), channel_id=1, source_target_pairs={{1,2},{2,1},{3,4},{4,3},{5,6},{6,5},{7,8},{8,7},{9,10},{10,9},{11,... | collective-permute-start | bytes 1769480 | tf_op jit(solution)/shard_map/ppermute | solution.py:26
  39.0 0.0 collective-permute-start.4
  39.0 17.2 %collective-permute-done.2.refs_2_ = bf16[768,1152]{1,0:T(8,128)(2,1)S(1)} collective-permute-done((bf16[768,1152]{1,0:T(8,128)(2,1)S(1)}, bf16[768,1152]{1,0:T(8,128)(2,1)S(1)}, u32[]{:S(2)}, u32[]{:S(2)}) %collective-permute-start.2) | collective-permute-done | bytes 1769504 | tf_op jit(solution)/shard_map/ppermute | solution.py:26
  56.1 6.2 %collective-permute-done.3.refs_3_ = bf16[768,1152]{1,0:T(8,128)(2,1)S(1)} collective-permute-done((bf16[768,1152]{1,0:T(8,128)(2,1)S(1)}, bf16[768,1152]{1,0:T(8,128)(2,1)S(1)}, u32[]{:S(2)}, u32[]{:S(2)}) %collective-permute-start.3) | collective-permute-done | bytes 1769504 | tf_op jit(solution)/shard_map/ppermute | solution.py:26
  62.4 2.1 %shard_map.64 = (bf16[1024,1152]{1,0:T(8,128)(2,1)S(1)}, bf16[1024,1152]{1,0:T(8,128)(2,1)S(1)}, bf16[512,1152]{1,0:T(8,128)(2,1)S(1)}, bf16[512,1152]{1,0:T(8,1...) custom-call(bf16[256,1152]{1,0:T(8,128)(2,1)S(1)} %get-tuple-element.33.refs_0_, ...), custom_call_target="tpu_custom_call" | custom-call | bytes 1024 | tf_op jit(solution)/shard_map/pallas_call | solution.py:246
  64.5 0.1 collective-permute-start.6
  64.6 7.4 %collective-permute-start.7 = (bf16[512,1152]{1,0:T(8,128)(2,1)S(1)}, bf16[512,1152]{1,0:T(8,128)(2,1)S(1)}, u32[]{:S(2)}, u32[]{:S(2)}) collective-permute-start(bf16[512,1152]{1,0:T(8,128)(2,1)S(1)} %get-tuple-element.46), channel_id=1, source_target_pairs={{1,2},{2,1},{3,4},{4,3},{5,6},{6,5},{7,8},{8,7},{9,10},{10,9},{11,... | collective-permute-start | bytes 3538952 | tf_op jit(solution)/shard_map/ppermute | solution.py:26
  72.0 5.9 %shard_map.65.refs_0_.sum_ref = f32[1024,1152]{1,0:T(8,128)S(1)} custom-call(f32[1]{0:T(128)S(6)} %exp.3.temper_ref, f32[1]{0:T(128)S(6)} %copy.33.offset_ref, bf16[1024,1152]{1,0:T(8,128)(2,1)S(1)} %get-tuple-element.28.own_unit, f32[1024,1152]{1,0:T(8,128)S(1)} %get-tuple-element.29.sum_ref, ...), custom_call_target="tpu_custom_call", output_to_operand_aliasing={{}: (3, {})} | custom-call | flops 7247757312 | bytes 4718592 | tf_op jit(solution)/shard_map/pallas_call | solution.py:288
  77.9 0.0 collective-permute-done.5.refs_4_
  77.9 0.0 collective-permute-done.4.refs_3_
  77.9 4.4 %collective-permute-start.8 = (bf16[256,1152]{1,0:T(8,128)(2,1)S(1)}, bf16[256,1152]{1,0:T(8,128)(2,1)S(1)}, u32[]{:S(2)}, u32[]{:S(2)}) collective-permute-start(bf16[256,1152]{1,0:T(8,128)(2,1)S(1)} %get-tuple-element.49), channel_id=1, source_target_pairs={{1,2},{2,1},{3,4},{4,3},{5,6},{6,5},{7,8},{8,7},{9,10},{10,9},{11,... | collective-permute-start | bytes 1769480 | tf_op jit(solution)/shard_map/ppermute | solution.py:26
  82.3 0.0 collective-permute-start.9
  82.3 5.9 %shard_map.67.sum_ref = f32[1024,1152]{1,0:T(8,128)S(1)} custom-call(f32[1]{0:T(128)S(6)} %exp.3.temper_ref, f32[1]{0:T(128)S(6)} %copy.33.offset_ref, bf16[1024,1152]{1,0:T(8,128)(2,1)S(1)} %get-tuple-element.41.own_unit, f32[1024,1152]{1,0:T(8,128)S(1)} %get-tuple-element.42.sum_ref, ...), custom_call_target="tpu_custom_call", output_to_operand_aliasing={{}: (3, {})} | custom-call | flops 7247757312 | bytes 4718592 | tf_op jit(solution)/shard_map/pallas_call | solution.py:288
  88.3 5.8 %collective-permute-done.6.middle = bf16[512,1152]{1,0:T(8,128)(2,1)S(1)} collective-permute-done((bf16[512,1152]{1,0:T(8,128)(2,1)S(1)}, bf16[512,1152]{1,0:T(8,128)(2,1)S(1)}, u32[]{:S(2)}, u32[]{:S(2)}) %collective-permute-start.6) | collective-permute-done | bytes 1179680 | tf_op jit(solution)/shard_map/ppermute | solution.py:26
  94.1 4.7 %shard_map.68.refs_0_.sum_ref = f32[1024,1152]{1,0:T(8,128)S(1)} custom-call(f32[1]{0:T(128)S(6)} %exp.3.temper_ref, f32[1]{0:T(128)S(6)} %copy.33.offset_ref, bf16[1024,1152]{1,0:T(8,128)(2,1)S(1)} %get-tuple-element.41.own_unit, f32[1024,1152]{1,0:T(8,128)S(1)} %shard_map.67.sum_ref, ...), custom_call_target="tpu_custom_call", output_to_operand_aliasing={{}: (3, {})} | custom-call | flops 9059696 | bytes 4718592 | tf_op jit(solution)/shard_map/pallas_call | solution.py:288
  98.7 1.6 %collective-permute-done.7.refs_1_ = bf16[512,1152]{1,0:T(8,128)(2,1)S(1)} collective-permute-done((bf16[512,1152]{1,0:T(8,128)(2,1)S(1)}, bf16[512,1152]{1,0:T(8,128)(2,1)S(1)}, u32[]{:S(2)}, u32[]{:S(2)}) %collective-permute-start.7) | collective-permute-done | bytes 1179680 | tf_op jit(solution)/shard_map/ppermute | solution.py:26
  100.3 4.7 %shard_map.70.refs_0_.sum_ref = f32[1024,1152]{1,0:T(8,128)S(1)} custom-call(f32[1]{0:T(128)S(6)} %exp.3.temper_ref, f32[1]{0:T(128)S(6)} %copy.33.offset_ref, bf16[1024,1152]{1,0:T(8,128)(2,1)S(1)} %get-tuple-element.28.own_unit, f32[1024,1152]{1,0:T(8,128)S(1)} %shard_map.65.refs_0_.sum_ref, ...), custom_call_target="tpu_custom_call", output_to_operand_aliasing={{}: (3, {})} | custom-call | flops 9059696 | bytes 4718592 | tf_op jit(solution)/shard_map/pallas_call | solution.py:288
  104.9 0.5 collective-permute-done.9.refs_1_
  105.5 4.2 %shard_map.72 = (f32[1024,1152]{1,0:T(8,128)}, f32[1024,1152]{1,0:T(8,128)}) custom-call(f32[1]{0:T(128)S(6)} %exp.3.temper_ref, f32[1]{0:T(128)S(6)} %copy.33.offset_ref, bf16[1024,1152]{1,0:T(8,128)(2,1)S(1)} %get-tuple-element.41.own_unit, f32[1024,1152]{1,0:T(8,128)S(1)} %shard_map.68.refs_0_.sum_ref, bf16[1024,1152]{1,0:T(8,128)(2,1)S(1)} %get-tuple-element.50.raw_ref, ...), custom_call_target="tpu_custom_call" | custom-call | flops 4831838208 | bytes 4718592 | tf_op jit(solution)/shard_map/pallas_call | solution.py:303
  109.6 2.6 %collective-permute-done.8.refs_0_ = bf16[256,1152]{1,0:T(8,128)(2,1)S(1)} collective-permute-done((bf16[256,1152]{1,0:T(8,128)(2,1)S(1)}, bf16[256,1152]{1,0:T(8,128)(2,1)S(1)}, u32[]{:S(2)}, u32[]{:S(2)}) %collective-permute-start.8) | collective-permute-done | bytes 589856 | tf_op jit(solution)/shard_map/ppermute | solution.py:26
  112.2 3.9 %shard_map.73 = (f32[1024,1152]{1,0:T(8,128)}, f32[1024,1152]{1,0:T(8,128)}) custom-call(f32[1]{0:T(128)S(6)} %exp.3.temper_ref, f32[1]{0:T(128)S(6)} %copy.33.offset_ref, bf16[1024,1152]{1,0:T(8,128)(2,1)S(1)} %get-tuple-element.28.own_unit, f32[1024,1152]{1,0:T(8,128)S(1)} %shard_map.70.refs_0_.sum_ref, ...), custom_call_target="tpu_custom_call", output_to_operand_aliasing={{0}: (7, {}), {1}: (8, {})} | custom-call | flops 4831838208 | bytes 4718592 | tf_op jit(solution)/shard_map/pallas_call | solution.py:303
  (4 shorter events, 0.0 us)
Async XLA Ops:
  1.9 30.1 %collective-permute-start = (bf16[256,1152]{1,0:T(8,128)(2,1)S(1)}, bf16[256,1152]{1,0:T(8,128)(2,1)S(1)}, u32[]{:S(2)}, u32[]{:S(2)}) collective-permute-start(bf16[256,1152]{1,0:T(8,128)(2,1)S(1)} %get-tuple-element.31.refs_0_), channel_id=1, source_target_pairs={{0,1},{1,0},{2,3},{3,2},{4,5},{5,4},{6,7},{7,6},{8,9},{9,8},{10,11... | collective-permute-start | bytes 1769480 | tf_op jit(solution)/shard_map/ppermute | solution.py:26
  3.7 28.3 %collective-permute-start.1 = (bf16[256,1152]{1,0:T(8,128)(2,1)S(1)}, bf16[256,1152]{1,0:T(8,128)(2,1)S(1)}, u32[]{:S(2)}, u32[]{:S(2)}) collective-permute-start(bf16[256,1152]{1,0:T(8,128)(2,1)S(1)} %shard_map.61), channel_id=1, source_target_pairs={{1,2},{2,1},{3,4},{4,3},{5,6},{6,5},{7,8},{8,7},{9,10},{10,9},{11,... | collective-permute-start | bytes 1769480 | tf_op jit(solution)/shard_map/ppermute | solution.py:26
  12.7 43.4 %collective-permute-start.2 = (bf16[768,1152]{1,0:T(8,128)(2,1)S(1)}, bf16[768,1152]{1,0:T(8,128)(2,1)S(1)}, u32[]{:S(2)}, u32[]{:S(2)}) collective-permute-start(bf16[768,1152]{1,0:T(8,128)(2,1)S(1)} %get-tuple-element.35), channel_id=1, source_target_pairs={{0,1},{1,0},{2,3},{3,2},{4,5},{5,4},{6,7},{7,6},{8,9},{9,8},{10,11... | collective-permute-start | bytes 5308424 | tf_op jit(solution)/shard_map/ppermute | solution.py:26
  12.8 49.6 %collective-permute-start.3 = (bf16[768,1152]{1,0:T(8,128)(2,1)S(1)}, bf16[768,1152]{1,0:T(8,128)(2,1)S(1)}, u32[]{:S(2)}, u32[]{:S(2)}) collective-permute-start(bf16[768,1152]{1,0:T(8,128)(2,1)S(1)} %get-tuple-element.36), channel_id=1, source_target_pairs={{1,2},{2,1},{3,4},{4,3},{5,6},{6,5},{7,8},{8,7},{9,10},{10,9},{11,... | collective-permute-start | bytes 5308424 | tf_op jit(solution)/shard_map/ppermute | solution.py:26
  32.6 45.3 %collective-permute-start.5 = (bf16[256,1152]{1,0:T(8,128)(2,1)S(1)}, bf16[256,1152]{1,0:T(8,128)(2,1)S(1)}, u32[]{:S(2)}, u32[]{:S(2)}) collective-permute-start(bf16[256,1152]{1,0:T(8,128)(2,1)S(1)} %get-tuple-element.33.refs_0_), channel_id=1, source_target_pairs={{1,2},{2,1},{3,4},{4,3},{5,6},{6,5},{7,8},{8,7},{9,10},{10,9},{11,... | collective-permute-start | bytes 1769480 | tf_op jit(solution)/shard_map/ppermute | solution.py:26
  39.0 39.0 %collective-permute-start.4 = (bf16[256,1152]{1,0:T(8,128)(2,1)S(1)}, bf16[256,1152]{1,0:T(8,128)(2,1)S(1)}, u32[]{:S(2)}, u32[]{:S(2)}) collective-permute-start(bf16[256,1152]{1,0:T(8,128)(2,1)S(1)} %get-tuple-element.34.refs_1_), channel_id=1, source_target_pairs={{0,1},{1,0},{2,3},{3,2},{4,5},{5,4},{6,7},{7,6},{8,9},{9,8},{10,11... | collective-permute-start | bytes 1769480 | tf_op jit(solution)/shard_map/ppermute | solution.py:26
  64.5 29.6 %collective-permute-start.6 = (bf16[512,1152]{1,0:T(8,128)(2,1)S(1)}, bf16[512,1152]{1,0:T(8,128)(2,1)S(1)}, u32[]{:S(2)}, u32[]{:S(2)}) collective-permute-start(bf16[512,1152]{1,0:T(8,128)(2,1)S(1)} %get-tuple-element.45), channel_id=1, source_target_pairs={{0,1},{1,0},{2,3},{3,2},{4,5},{5,4},{6,7},{7,6},{8,9},{9,8},{10,11... | collective-permute-start | bytes 3538952 | tf_op jit(solution)/shard_map/ppermute | solution.py:26
  64.6 35.7 %collective-permute-start.7 = (bf16[512,1152]{1,0:T(8,128)(2,1)S(1)}, bf16[512,1152]{1,0:T(8,128)(2,1)S(1)}, u32[]{:S(2)}, u32[]{:S(2)}) collective-permute-start(bf16[512,1152]{1,0:T(8,128)(2,1)S(1)} %get-tuple-element.46), channel_id=1, source_target_pairs={{1,2},{2,1},{3,4},{4,3},{5,6},{6,5},{7,8},{8,7},{9,10},{10,9},{11,... | collective-permute-start | bytes 3538952 | tf_op jit(solution)/shard_map/ppermute | solution.py:26
  77.9 34.3 %collective-permute-start.8 = (bf16[256,1152]{1,0:T(8,128)(2,1)S(1)}, bf16[256,1152]{1,0:T(8,128)(2,1)S(1)}, u32[]{:S(2)}, u32[]{:S(2)}) collective-permute-start(bf16[256,1152]{1,0:T(8,128)(2,1)S(1)} %get-tuple-element.49), channel_id=1, source_target_pairs={{1,2},{2,1},{3,4},{4,3},{5,6},{6,5},{7,8},{8,7},{9,10},{10,9},{11,... | collective-permute-start | bytes 1769480 | tf_op jit(solution)/shard_map/ppermute | solution.py:26
  82.3 23.1 %collective-permute-start.9 = (bf16[256,1152]{1,0:T(8,128)(2,1)S(1)}, bf16[256,1152]{1,0:T(8,128)(2,1)S(1)}, u32[]{:S(2)}, u32[]{:S(2)}) collective-permute-start(bf16[256,1152]{1,0:T(8,128)(2,1)S(1)} %get-tuple-element.51), channel_id=1, source_target_pairs={{0,1},{1,0},{2,3},{3,2},{4,5},{5,4},{6,7},{7,6},{8,9},{9,8},{10,11... | collective-permute-start | bytes 1769480 | tf_op jit(solution)/shard_map/ppermute | solution.py:26

commit v4 on v3

--- a/solution.py
+++ b/solution.py
@@ -13,6 +13,7 @@
 start = 256
 split = 768
 tile = 256
+last_tiles = (128, 256, 256, 256, 128)
 lanes = 128
 
 
@@ -23,6 +24,12 @@
     for low in range(first, count, 2):
         high = (low + 1) % count
         pairs += [(low, high), (high, low)]
+    return lax.ppermute(value, axes, pairs)
+
+
+def passed_along(value, steps):
+    count = lax.axis_size(axes)
+    pairs = [(source, (source + steps) % count) for source in range(count)]
     return lax.ppermute(value, axes, pairs)
 
 
@@ -63,8 +70,8 @@
     return weights.astype(jnp.bfloat16)
 
 
-def attend(own_unit, others, temper, offset, sum_ref, finish):
-    tiles = [pl.ds(first, tile) for first in range(0, own_unit.shape[0], tile)]
+def attend(own_unit, others, temper, offset, sum_ref, finish, sizes=(tile,) * 4):
+    tiles = [pl.ds(sum(sizes[:i]), size) for i, size in enumerate(sizes)]
     ahead = weigh(own_unit[tiles[0], :], others[...], temper, offset)
     for rows, following in zip(tiles, tiles[1:] + [None]):
         weights = ahead
@@ -76,7 +83,7 @@
         )
 
 
-def pieces_kernel(first, img_ref, txt_ref, *refs):
+def pieces_kernel(first, by_name, img_ref, txt_ref, *refs):
     inner_ref, outer_ref, sems = refs[-3:]
     rows = pl.ds(first, inner_ref.shape[0])
 
@@ -90,16 +97,22 @@
         for copy in copies:
             copy.wait()
 
-    on_even(lambda: fetch(txt_ref, img_ref), lambda: fetch(img_ref, txt_ref))
+    if by_name:
+        on_even(lambda: fetch(txt_ref, img_ref), lambda: fetch(img_ref, txt_ref))
+    else:
+        fetch(txt_ref, img_ref)
 
 
 def gate_kernel(*refs):
     del refs
 
 
-def first_kernel(token_ref, inner_ref, outer_ref, inner_unit, outer_unit):
-    unit_rows(inner_ref, inner_unit)
-    unit_rows(outer_ref, outer_unit)
+def first_kernel(token_ref, txt_ref, img_ref, inner_unit, outer_unit):
+    def take(inner_ref, outer_ref):
+        unit_rows(inner_ref, inner_unit)
+        unit_rows(outer_ref, outer_unit)
+
+    on_even(lambda: take(img_ref, txt_ref), lambda: take(txt_ref, img_ref))
 
 
 def rest_kernel(*refs):
@@ -161,30 +174,26 @@
     grad_img, grad_txt, ready, sems = refs
     temper = temper_ref[0]
 
-    def copies(into, rows):
-        return pltpu.make_async_copy(
-            ready.at[rows, :], into.at[rows, :], sems.at[rows.start // tile]
-        )
-
-    def on_target(do):
-        into_txt, into_img = functools.partial(do, grad_txt), functools.partial(do, grad_img)
-        on_even(into_txt, into_img) if inner else on_even(into_img, into_txt)
-
-    def finish(rows, total):
-        raw = raw_ref[rows, :].astype(jnp.float32)
-        inverse = inverse_ref[rows, :1]
-        scale = temper * inverse
-        along = jnp.sum(raw * total, axis=1, keepdims=True)
-        ready[rows, :] = scale * total - (scale * inverse * inverse * along) * raw
-        on_target(lambda into: copies(into, rows).start())
-
-    attend(own_unit, others, temper, offset_ref[0], sum_ref, finish)
-
-    def wait(into):
-        for first in range(0, own_unit.shape[0], tile):
-            copies(into, pl.ds(first, tile)).wait()
-
-    on_target(wait)
+    def run(into):
+        copies = []
+
+        def finish(rows, total):
+            raw = raw_ref[rows, :].astype(jnp.float32)
+            inverse = inverse_ref[rows, :1]
+            scale = temper * inverse
+            along = jnp.sum(raw * total, axis=1, keepdims=True)
+            ready[rows, :] = scale * total - (scale * inverse * inverse * along) * raw
+            copies.append(
+                pltpu.make_async_copy(ready.at[rows, :], into.at[rows, :], sems.at[len(copies)])
+            )
+            copies[-1].start()
+
+        attend(own_unit, others, temper, offset_ref[0], sum_ref, finish, last_tiles)
+        for copy in copies:
+            copy.wait()
+
+    into_txt, into_img = functools.partial(run, grad_txt), functools.partial(run, grad_img)
+    on_even(into_txt, into_img) if inner else on_even(into_img, into_txt)
 
 
 scalar = pl.BlockSpec(memory_space=pltpu.SMEM)
@@ -218,7 +227,7 @@
 
 def pieces_of(images, texts, first, last, tokens):
     return pl.pallas_call(
-        functools.partial(pieces_kernel, first),
+        functools.partial(pieces_kernel, first, bool(tokens)),
         in_specs=[off_chip] * 2 + [anywhere] * len(tokens),
         out_specs=[on_chip] * 2,
         out_shape=[held(last - first, images)] * 2,
@@ -228,15 +237,15 @@
     )(*pinned(images, texts, memory=pltpu.HBM), *tokens)
 
 
-def first_units(token, inner, outer):
+def first_units(token, texts, images):
     return pl.pallas_call(
         first_kernel,
         in_specs=[anywhere] + [on_chip] * 2,
         out_specs=[on_chip] * 2,
-        out_shape=[held(inner.shape[0], inner)] * 2,
+        out_shape=[held(texts.shape[0], texts)] * 2,
         compiler_params=limit(4),
         cost_estimate=small,
-    )(token, *pinned(inner, outer))
+    )(token, *pinned(texts, images))
 
 
 def rest_units(firsts, rests):
@@ -308,7 +317,7 @@
         input_output_aliases={} if inner else {7: 0, 8: 1},
         scratch_shapes=[
             pltpu.VMEM((rows, width), jnp.float32),
-            pltpu.SemaphoreType.DMA((rows // tile,)),
+            pltpu.SemaphoreType.DMA((len(last_tiles),)),
         ],
         compiler_params=limit(16),
         cost_estimate=costs(rows, piece.shape[0], width, 16),
@@ -320,7 +329,7 @@
     rows = images.shape[0]
     pieces = pieces_of(images, texts, 0, start, [])
     pieces = [pieces[0], gate(pieces[0], pieces[1])[0]]
-    firsts = [exchanged(pieces[0], True), exchanged(pieces[1], False)]
+    firsts = [passed_along(pieces[0], 1), passed_along(pieces[1], -1)]
     pieces = pieces_of(images, texts, start, rows, pieces[:1])
     rests = [exchanged(pieces[0], True), exchanged(pieces[1], False)]
     raw_inner, raw_outer, sum_inner, sum_outer, unit_inner, unit_outer, inv_inner, inv_outer = (

time: 117 us -> 116 us (level)
    ppermute x10 -> x8, starting transfers between devices: 28.1 us -> 19.3 us  [exchanged(): return lax.ppermute(value, axes, pairs)]
    ppermute x0 -> x2, starting transfers between devices: none -> 8.37 us  [passed_along(): return lax.ppermute(value, axes, pairs)]
    ppermute x10 -> x8, waiting for transfers between devices: 33.8 us -> 33.9 us  [exchanged(): return lax.ppermute(value, axes, pairs)]
  transfers between devices with their start and end apart: 10 -> 10, of which waited for: 6 -> 5; matrix products, arithmetic and copies ran while one was open for 0% -> 0% of each run, Pallas kernels for 40% -> 40%
where the time goes in v4:
time: 116 us
  Pallas kernels  51.9 us (45%)
  waiting for transfers between devices  33.9 us (29%)
  starting transfers between devices  27.7 us (24%)
  between operations  2.29 us (2%)
    ppermute x8, waiting for transfers between devices, exchanged(): return lax.ppermute(value, axes, pairs)  33.9 us
    pallas_call x4, Pallas kernels, more_block(): pl.pallas_call(far_kernel if several else near_kernel, in_specs=[scalar]...  21.2 us
    ppermute x8, starting transfers between devices, exchanged(): return lax.ppermute(value, axes, pairs)  19.3 us
    pallas_call x1, Pallas kernels, own_block(): pl.pallas_call(own_kernel, in_specs=[scalar] * 2 + [off_chip] * 2, out_sp...  16.9 us
    ppermute x2, starting transfers between devices, passed_along(): return lax.ppermute(value, axes, pairs)  8.37 us
    pallas_call x2, Pallas kernels, last_block(): pl.pallas_call(functools.partial(last_kernel, inner), in_specs=[scalar] *...  7.78 us
    pallas_call x2, Pallas kernels, pieces_of(): pl.pallas_call(functools.partial(pieces_kernel, first, bool(tokens)), in_...  3.29 us
  transfers between devices with their start and end apart: 10, of which 5 were waited for; matrix products, arithmetic and copies ran while one was open for 0% of the time, Pallas kernels for 40%

profile of v4, /device:TPU:0, one launch (start us, length us, event | category | flops | bytes accessed | tf_op | source)
XLA Modules:
  0.0 115.8 jit_solution(10720526197184044045)
XLA Ops:
  0.6 1.3 %shard_map.60 = (bf16[256,1152]{1,0:T(8,128)(2,1)S(1)}, bf16[256,1152]{1,0:T(8,128)(2,1)S(1)}) custom-call(bf16[1024,1152]{1,0:T(8,128)(2,1)} %img_ref.5, bf16[1024,1152]{1,0:T(8,128)(2,1)} %txt_ref.5), custom_call_target="tpu_custom_call" | custom-call | bytes 1024 | tf_op jit(solution)/shard_map/pallas_call | solution.py:229
  1.9 1.7 %collective-permute-start = (bf16[256,1152]{1,0:T(8,128)(2,1)S(1)}, bf16[256,1152]{1,0:T(8,128)(2,1)S(1)}, u32[]{:S(2)}, u32[]{:S(2)}) collective-permute-start(bf16[256,1152]{1,0:T(8,128)(2,1)S(1)} %get-tuple-element.31.refs_0_), channel_id=1, source_target_pairs={{0,1},{1,2},{2,3},{3,4},{4,5},{5,6},{6,7},{7,8},{8,9},{9,10},{10,1... | collective-permute-start | bytes 1769480 | tf_op jit(solution)/shard_map/ppermute | solution.py:33
  3.6 6.6 %collective-permute-start.1 = (bf16[256,1152]{1,0:T(8,128)(2,1)S(1)}, bf16[256,1152]{1,0:T(8,128)(2,1)S(1)}, u32[]{:S(2)}, u32[]{:S(2)}) collective-permute-start(bf16[256,1152]{1,0:T(8,128)(2,1)S(1)} %shard_map.61), channel_id=1, source_target_pairs={{0,127},{1,0},{2,1},{3,2},{4,3},{5,4},{6,5},{7,6},{8,7},{9,8},{10,... | collective-permute-start | bytes 1769480 | tf_op jit(solution)/shard_map/ppermute | solution.py:33
  10.3 2.0 %shard_map.63 = (bf16[768,1152]{1,0:T(8,128)(2,1)S(1)}, bf16[768,1152]{1,0:T(8,128)(2,1)S(1)}) custom-call(bf16[1024,1152]{1,0:T(8,128)(2,1)} %img_ref.5, bf16[1024,1152]{1,0:T(8,128)(2,1)} %txt_ref.5, bf16[256,1152]{1,0:T(8,128)(2,1)S(1)} %get-tuple-element.31.refs_0_), custom_call_target="tpu_custom_call" | custom-call | bytes 1024 | tf_op jit(solution)/shard_map/pallas_call | solution.py:229
  12.3 0.1 collective-permute-start.2
  12.4 1.8 %collective-permute-start.3 = (bf16[768,1152]{1,0:T(8,128)(2,1)S(1)}, bf16[768,1152]{1,0:T(8,128)(2,1)S(1)}, u32[]{:S(2)}, u32[]{:S(2)}) collective-permute-start(bf16[768,1152]{1,0:T(8,128)(2,1)S(1)} %get-tuple-element.36), channel_id=1, source_target_pairs={{1,2},{2,1},{3,4},{4,3},{5,6},{6,5},{7,8},{8,7},{9,10},{10,9},{11,... | collective-permute-start | bytes 5308424 | tf_op jit(solution)/shard_map/ppermute | solution.py:27
  15.6 16.9 %shard_map.59 = (bf16[1024,1152]{1,0:T(8,128)(2,1)S(1)}, bf16[1024,1152]{1,0:T(8,128)(2,1)S(1)}, f32[1024,1152]{1,0:T(8,128)S(1)}, f32[1024,1152]{1,0:T(8,128)S(...) custom-call(f32[1]{0:T(128)S(6)} %exp.3.temper_ref, ...), custom_call_target="tpu_custom_call" | custom-call | flops 38654705664 | bytes 4718592 | tf_op jit(solution)/shard_map/pallas_call | solution.py:282
  32.4 0.0 collective-permute-done.1.img_ref
  32.4 0.0 collective-permute-done.txt_ref
  32.5 0.6 shard_map.62
  33.1 5.5 %collective-permute-start.5 = (bf16[256,1152]{1,0:T(8,128)(2,1)S(1)}, bf16[256,1152]{1,0:T(8,128)(2,1)S(1)}, u32[]{:S(2)}, u32[]{:S(2)}) collective-permute-start(bf16[256,1152]{1,0:T(8,128)(2,1)S(1)} %get-tuple-element.33.refs_0_), channel_id=1, source_target_pairs={{1,2},{2,1},{3,4},{4,3},{5,6},{6,5},{7,8},{8,7},{9,10},{10,9},{11,... | collective-permute-start | bytes 1769480 | tf_op jit(solution)/shard_map/ppermute | solution.py:27
  38.6 0.0 collective-permute-start.4
  38.6 19.2 %collective-permute-done.2.refs_2_ = bf16[768,1152]{1,0:T(8,128)(2,1)S(1)} collective-permute-done((bf16[768,1152]{1,0:T(8,128)(2,1)S(1)}, bf16[768,1152]{1,0:T(8,128)(2,1)S(1)}, u32[]{:S(2)}, u32[]{:S(2)}) %collective-permute-start.2) | collective-permute-done | bytes 1769504 | tf_op jit(solution)/shard_map/ppermute | solution.py:27
  57.8 4.2 %collective-permute-done.3.refs_3_ = bf16[768,1152]{1,0:T(8,128)(2,1)S(1)} collective-permute-done((bf16[768,1152]{1,0:T(8,128)(2,1)S(1)}, bf16[768,1152]{1,0:T(8,128)(2,1)S(1)}, u32[]{:S(2)}, u32[]{:S(2)}) %collective-permute-start.3) | collective-permute-done | bytes 1769504 | tf_op jit(solution)/shard_map/ppermute | solution.py:27
  62.0 2.1 %shard_map.64 = (bf16[1024,1152]{1,0:T(8,128)(2,1)S(1)}, bf16[1024,1152]{1,0:T(8,128)(2,1)S(1)}, bf16[512,1152]{1,0:T(8,128)(2,1)S(1)}, bf16[512,1152]{1,0:T(8,1...) custom-call(bf16[256,1152]{1,0:T(8,128)(2,1)S(1)} %get-tuple-element.33.refs_0_, ...), custom_call_target="tpu_custom_call" | custom-call | bytes 1024 | tf_op jit(solution)/shard_map/pallas_call | solution.py:255
  64.1 0.1 collective-permute-start.6
  64.2 7.4 %collective-permute-start.7 = (bf16[512,1152]{1,0:T(8,128)(2,1)S(1)}, bf16[512,1152]{1,0:T(8,128)(2,1)S(1)}, u32[]{:S(2)}, u32[]{:S(2)}) collective-permute-start(bf16[512,1152]{1,0:T(8,128)(2,1)S(1)} %get-tuple-element.46), channel_id=1, source_target_pairs={{1,2},{2,1},{3,4},{4,3},{5,6},{6,5},{7,8},{8,7},{9,10},{10,9},{11,... | collective-permute-start | bytes 3538952 | tf_op jit(solution)/shard_map/ppermute | solution.py:27
  71.6 5.9 %shard_map.65.refs_0_.sum_ref = f32[1024,1152]{1,0:T(8,128)S(1)} custom-call(f32[1]{0:T(128)S(6)} %exp.3.temper_ref, f32[1]{0:T(128)S(6)} %copy.33.offset_ref, bf16[1024,1152]{1,0:T(8,128)(2,1)S(1)} %get-tuple-element.28.own_unit, f32[1024,1152]{1,0:T(8,128)S(1)} %get-tuple-element.29.sum_ref, ...), custom_call_target="tpu_custom_call", output_to_operand_aliasing={{}: (3, {})} | custom-call | flops 7247757312 | bytes 4718592 | tf_op jit(solution)/shard_map/pallas_call | solution.py:297
  77.5 0.0 collective-permute-done.5.refs_4_
  77.5 0.0 collective-permute-done.4.refs_3_
  77.6 4.4 %collective-permute-start.8 = (bf16[256,1152]{1,0:T(8,128)(2,1)S(1)}, bf16[256,1152]{1,0:T(8,128)(2,1)S(1)}, u32[]{:S(2)}, u32[]{:S(2)}) collective-permute-start(bf16[256,1152]{1,0:T(8,128)(2,1)S(1)} %get-tuple-element.49), channel_id=1, source_target_pairs={{1,2},{2,1},{3,4},{4,3},{5,6},{6,5},{7,8},{8,7},{9,10},{10,9},{11,... | collective-permute-start | bytes 1769480 | tf_op jit(solution)/shard_map/ppermute | solution.py:27
  82.0 0.0 collective-permute-start.9
  82.0 5.9 %shard_map.67.sum_ref = f32[1024,1152]{1,0:T(8,128)S(1)} custom-call(f32[1]{0:T(128)S(6)} %exp.3.temper_ref, f32[1]{0:T(128)S(6)} %copy.33.offset_ref, bf16[1024,1152]{1,0:T(8,128)(2,1)S(1)} %get-tuple-element.41.own_unit, f32[1024,1152]{1,0:T(8,128)S(1)} %get-tuple-element.42.sum_ref, ...), custom_call_target="tpu_custom_call", output_to_operand_aliasing={{}: (3, {})} | custom-call | flops 7247757312 | bytes 4718592 | tf_op jit(solution)/shard_map/pallas_call | solution.py:297
  87.9 7.8 %collective-permute-done.6.middle = bf16[512,1152]{1,0:T(8,128)(2,1)S(1)} collective-permute-done((bf16[512,1152]{1,0:T(8,128)(2,1)S(1)}, bf16[512,1152]{1,0:T(8,128)(2,1)S(1)}, u32[]{:S(2)}, u32[]{:S(2)}) %collective-permute-start.6) | collective-permute-done | bytes 1179680 | tf_op jit(solution)/shard_map/ppermute | solution.py:27
  95.7 4.7 %shard_map.68.refs_0_.sum_ref = f32[1024,1152]{1,0:T(8,128)S(1)} custom-call(f32[1]{0:T(128)S(6)} %exp.3.temper_ref, f32[1]{0:T(128)S(6)} %copy.33.offset_ref, bf16[1024,1152]{1,0:T(8,128)(2,1)S(1)} %get-tuple-element.41.own_unit, f32[1024,1152]{1,0:T(8,128)S(1)} %shard_map.67.sum_ref, ...), custom_call_target="tpu_custom_call", output_to_operand_aliasing={{}: (3, {})} | custom-call | flops 9059696 | bytes 4718592 | tf_op jit(solution)/shard_map/pallas_call | solution.py:297
  100.4 0.0 collective-permute-done.7.refs_1_
  100.4 4.7 %shard_map.70.refs_0_.sum_ref = f32[1024,1152]{1,0:T(8,128)S(1)} custom-call(f32[1]{0:T(128)S(6)} %exp.3.temper_ref, f32[1]{0:T(128)S(6)} %copy.33.offset_ref, bf16[1024,1152]{1,0:T(8,128)(2,1)S(1)} %get-tuple-element.28.own_unit, f32[1024,1152]{1,0:T(8,128)S(1)} %shard_map.65.refs_0_.sum_ref, ...), custom_call_target="tpu_custom_call", output_to_operand_aliasing={{}: (3, {})} | custom-call | flops 9059696 | bytes 4718592 | tf_op jit(solution)/shard_map/pallas_call | solution.py:297
  105.1 1.8 %collective-permute-done.9.refs_1_ = bf16[256,1152]{1,0:T(8,128)(2,1)S(1)} collective-permute-done((bf16[256,1152]{1,0:T(8,128)(2,1)S(1)}, bf16[256,1152]{1,0:T(8,128)(2,1)S(1)}, u32[]{:S(2)}, u32[]{:S(2)}) %collective-permute-start.9) | collective-permute-done | bytes 589856 | tf_op jit(solution)/shard_map/ppermute | solution.py:27
  106.9 3.9 %shard_map.72 = (f32[1024,1152]{1,0:T(8,128)}, f32[1024,1152]{1,0:T(8,128)}) custom-call(f32[1]{0:T(128)S(6)} %exp.3.temper_ref, f32[1]{0:T(128)S(6)} %copy.33.offset_ref, bf16[1024,1152]{1,0:T(8,128)(2,1)S(1)} %get-tuple-element.41.own_unit, f32[1024,1152]{1,0:T(8,128)S(1)} %shard_map.68.refs_0_.sum_ref, bf16[1024,1152]{1,0:T(8,128)(2,1)S(1)} %get-tuple-element.50.raw_ref, ...), custom_call_target="tpu_custom_call" | custom-call | flops 4831838208 | bytes 4718592 | tf_op jit(solution)/shard_map/pallas_call | solution.py:312
  110.8 0.9 collective-permute-done.8.refs_0_
  111.7 3.9 %shard_map.73 = (f32[1024,1152]{1,0:T(8,128)}, f32[1024,1152]{1,0:T(8,128)}) custom-call(f32[1]{0:T(128)S(6)} %exp.3.temper_ref, f32[1]{0:T(128)S(6)} %copy.33.offset_ref, bf16[1024,1152]{1,0:T(8,128)(2,1)S(1)} %get-tuple-element.28.own_unit, f32[1024,1152]{1,0:T(8,128)S(1)} %shard_map.70.refs_0_.sum_ref, ...), custom_call_target="tpu_custom_call", output_to_operand_aliasing={{0}: (7, {}), {1}: (8, {})} | custom-call | flops 4831838208 | bytes 4718592 | tf_op jit(solution)/shard_map/pallas_call | solution.py:312
  (4 shorter events, 0.0 us)
Async XLA Ops:
  1.9 30.6 %collective-permute-start = (bf16[256,1152]{1,0:T(8,128)(2,1)S(1)}, bf16[256,1152]{1,0:T(8,128)(2,1)S(1)}, u32[]{:S(2)}, u32[]{:S(2)}) collective-permute-start(bf16[256,1152]{1,0:T(8,128)(2,1)S(1)} %get-tuple-element.31.refs_0_), channel_id=1, source_target_pairs={{0,1},{1,2},{2,3},{3,4},{4,5},{5,6},{6,7},{7,8},{8,9},{9,10},{10,1... | collective-permute-start | bytes 1769480 | tf_op jit(solution)/shard_map/ppermute | solution.py:33
  3.6 28.8 %collective-permute-start.1 = (bf16[256,1152]{1,0:T(8,128)(2,1)S(1)}, bf16[256,1152]{1,0:T(8,128)(2,1)S(1)}, u32[]{:S(2)}, u32[]{:S(2)}) collective-permute-start(bf16[256,1152]{1,0:T(8,128)(2,1)S(1)} %shard_map.61), channel_id=1, source_target_pairs={{0,127},{1,0},{2,1},{3,2},{4,3},{5,4},{6,5},{7,6},{8,7},{9,8},{10,... | collective-permute-start | bytes 1769480 | tf_op jit(solution)/shard_map/ppermute | solution.py:33
  12.3 45.5 %collective-permute-start.2 = (bf16[768,1152]{1,0:T(8,128)(2,1)S(1)}, bf16[768,1152]{1,0:T(8,128)(2,1)S(1)}, u32[]{:S(2)}, u32[]{:S(2)}) collective-permute-start(bf16[768,1152]{1,0:T(8,128)(2,1)S(1)} %get-tuple-element.35), channel_id=1, source_target_pairs={{0,1},{1,0},{2,3},{3,2},{4,5},{5,4},{6,7},{7,6},{8,9},{9,8},{10,11... | collective-permute-start | bytes 5308424 | tf_op jit(solution)/shard_map/ppermute | solution.py:27
  12.4 49.6 %collective-permute-start.3 = (bf16[768,1152]{1,0:T(8,128)(2,1)S(1)}, bf16[768,1152]{1,0:T(8,128)(2,1)S(1)}, u32[]{:S(2)}, u32[]{:S(2)}) collective-permute-start(bf16[768,1152]{1,0:T(8,128)(2,1)S(1)} %get-tuple-element.36), channel_id=1, source_target_pairs={{1,2},{2,1},{3,4},{4,3},{5,6},{6,5},{7,8},{8,7},{9,10},{10,9},{11,... | collective-permute-start | bytes 5308424 | tf_op jit(solution)/shard_map/ppermute | solution.py:27
  33.1 44.5 %collective-permute-start.5 = (bf16[256,1152]{1,0:T(8,128)(2,1)S(1)}, bf16[256,1152]{1,0:T(8,128)(2,1)S(1)}, u32[]{:S(2)}, u32[]{:S(2)}) collective-permute-start(bf16[256,1152]{1,0:T(8,128)(2,1)S(1)} %get-tuple-element.33.refs_0_), channel_id=1, source_target_pairs={{1,2},{2,1},{3,4},{4,3},{5,6},{6,5},{7,8},{8,7},{9,10},{10,9},{11,... | collective-permute-start | bytes 1769480 | tf_op jit(solution)/shard_map/ppermute | solution.py:27
  38.6 39.0 %collective-permute-start.4 = (bf16[256,1152]{1,0:T(8,128)(2,1)S(1)}, bf16[256,1152]{1,0:T(8,128)(2,1)S(1)}, u32[]{:S(2)}, u32[]{:S(2)}) collective-permute-start(bf16[256,1152]{1,0:T(8,128)(2,1)S(1)} %get-tuple-element.34.refs_1_), channel_id=1, source_target_pairs={{0,1},{1,0},{2,3},{3,2},{4,5},{5,4},{6,7},{7,6},{8,9},{9,8},{10,11... | collective-permute-start | bytes 1769480 | tf_op jit(solution)/shard_map/ppermute | solution.py:27
  64.1 31.6 %collective-permute-start.6 = (bf16[512,1152]{1,0:T(8,128)(2,1)S(1)}, bf16[512,1152]{1,0:T(8,128)(2,1)S(1)}, u32[]{:S(2)}, u32[]{:S(2)}) collective-permute-start(bf16[512,1152]{1,0:T(8,128)(2,1)S(1)} %get-tuple-element.45), channel_id=1, source_target_pairs={{0,1},{1,0},{2,3},{3,2},{4,5},{5,4},{6,7},{7,6},{8,9},{9,8},{10,11... | collective-permute-start | bytes 3538952 | tf_op jit(solution)/shard_map/ppermute | solution.py:27
  64.2 36.2 %collective-permute-start.7 = (bf16[512,1152]{1,0:T(8,128)(2,1)S(1)}, bf16[512,1152]{1,0:T(8,128)(2,1)S(1)}, u32[]{:S(2)}, u32[]{:S(2)}) collective-permute-start(bf16[512,1152]{1,0:T(8,128)(2,1)S(1)} %get-tuple-element.46), channel_id=1, source_target_pairs={{1,2},{2,1},{3,4},{4,3},{5,6},{6,5},{7,8},{8,7},{9,10},{10,9},{11,... | collective-permute-start | bytes 3538952 | tf_op jit(solution)/shard_map/ppermute | solution.py:27
  77.6 34.1 %collective-permute-start.8 = (bf16[256,1152]{1,0:T(8,128)(2,1)S(1)}, bf16[256,1152]{1,0:T(8,128)(2,1)S(1)}, u32[]{:S(2)}, u32[]{:S(2)}) collective-permute-start(bf16[256,1152]{1,0:T(8,128)(2,1)S(1)} %get-tuple-element.49), channel_id=1, source_target_pairs={{1,2},{2,1},{3,4},{4,3},{5,6},{6,5},{7,8},{8,7},{9,10},{10,9},{11,... | collective-permute-start | bytes 1769480 | tf_op jit(solution)/shard_map/ppermute | solution.py:27
  82.0 24.9 %collective-permute-start.9 = (bf16[256,1152]{1,0:T(8,128)(2,1)S(1)}, bf16[256,1152]{1,0:T(8,128)(2,1)S(1)}, u32[]{:S(2)}, u32[]{:S(2)}) collective-permute-start(bf16[256,1152]{1,0:T(8,128)(2,1)S(1)} %get-tuple-element.51), channel_id=1, source_target_pairs={{0,1},{1,0},{2,3},{3,2},{4,5},{5,4},{6,7},{7,6},{8,9},{9,8},{10,11... | collective-permute-start | bytes 1769480 | tf_op jit(solution)/shard_map/ppermute | solution.py:27

commit v5 on v4

--- a/solution.py
+++ b/solution.py
@@ -24,12 +24,6 @@
     for low in range(first, count, 2):
         high = (low + 1) % count
         pairs += [(low, high), (high, low)]
-    return lax.ppermute(value, axes, pairs)
-
-
-def passed_along(value, steps):
-    count = lax.axis_size(axes)
-    pairs = [(source, (source + steps) % count) for source in range(count)]
     return lax.ppermute(value, axes, pairs)
 
 
@@ -83,7 +77,7 @@
         )
 
 
-def pieces_kernel(first, by_name, img_ref, txt_ref, *refs):
+def pieces_kernel(first, img_ref, txt_ref, *refs):
     inner_ref, outer_ref, sems = refs[-3:]
     rows = pl.ds(first, inner_ref.shape[0])
 
@@ -97,22 +91,16 @@
         for copy in copies:
             copy.wait()
 
-    if by_name:
-        on_even(lambda: fetch(txt_ref, img_ref), lambda: fetch(img_ref, txt_ref))
-    else:
-        fetch(txt_ref, img_ref)
+    on_even(lambda: fetch(txt_ref, img_ref), lambda: fetch(img_ref, txt_ref))
 
 
 def gate_kernel(*refs):
     del refs
 
 
-def first_kernel(token_ref, txt_ref, img_ref, inner_unit, outer_unit):
-    def take(inner_ref, outer_ref):
-        unit_rows(inner_ref, inner_unit)
-        unit_rows(outer_ref, outer_unit)
-
-    on_even(lambda: take(img_ref, txt_ref), lambda: take(txt_ref, img_ref))
+def first_kernel(token_ref, inner_ref, outer_ref, inner_unit, outer_unit):
+    unit_rows(inner_ref, inner_unit)
+    unit_rows(outer_ref, outer_unit)
 
 
 def rest_kernel(*refs):
@@ -227,7 +215,7 @@
 
 def pieces_of(images, texts, first, last, tokens):
     return pl.pallas_call(
-        functools.partial(pieces_kernel, first, bool(tokens)),
+        functools.partial(pieces_kernel, first),
         in_specs=[off_chip] * 2 + [anywhere] * len(tokens),
         out_specs=[on_chip] * 2,
         out_shape=[held(last - first, images)] * 2,
@@ -237,15 +225,15 @@
     )(*pinned(images, texts, memory=pltpu.HBM), *tokens)
 
 
-def first_units(token, texts, images):
+def first_units(token, inner, outer):
     return pl.pallas_call(
         first_kernel,
         in_specs=[anywhere] + [on_chip] * 2,
         out_specs=[on_chip] * 2,
-        out_shape=[held(texts.shape[0], texts)] * 2,
+        out_shape=[held(inner.shape[0], inner)] * 2,
         compiler_params=limit(4),
         cost_estimate=small,
-    )(token, *pinned(texts, images))
+    )(token, *pinned(inner, outer))
 
 
 def rest_units(firsts, rests):
@@ -329,7 +317,7 @@
     rows = images.shape[0]
     pieces = pieces_of(images, texts, 0, start, [])
     pieces = [pieces[0], gate(pieces[0], pieces[1])[0]]
-    firsts = [passed_along(pieces[0], 1), passed_along(pieces[1], -1)]
+    firsts = [exchanged(pieces[0], True), exchanged(pieces[1], False)]
     pieces = pieces_of(images, texts, start, rows, pieces[:1])
     rests = [exchanged(pieces[0], True), exchanged(pieces[1], False)]
     raw_inner, raw_outer, sum_inner, sum_outer, unit_inner, unit_outer, inv_inner, inv_outer = (

time: 116 us -> 116 us (level)
    ppermute x8 -> x10, starting transfers between devices: 19.3 us -> 28.1 us  [exchanged(): return lax.ppermute(value, axes, pairs)]
    ppermute x2 -> x0, starting transfers between devices: 8.37 us -> none  [passed_along(): return lax.ppermute(value, axes, pairs)]
    ppermute x8 -> x10, waiting for transfers between devices: 33.9 us -> 34.1 us  [exchanged(): return lax.ppermute(value, axes, pairs)]
  transfers between devices with their start and end apart: 10 -> 10, of which waited for: 5 -> 6; matrix products, arithmetic and copies ran while one was open for 0% -> 0% of each run, Pallas kernels for 40% -> 40%
where the time goes in v5:
time: 116 us
  Pallas kernels  51.8 us (45%)
  waiting for transfers between devices  34.1 us (29%)
  starting transfers between devices  28.1 us (24%)
  between operations  2.27 us (2%)
    ppermute x10, waiting for transfers between devices, exchanged(): return lax.ppermute(value, axes, pairs)  34.1 us
    ppermute x10, starting transfers between devices, exchanged(): return lax.ppermute(value, axes, pairs)  28.1 us
    pallas_call x4, Pallas kernels, more_block(): pl.pallas_call(far_kernel if several else near_kernel, in_specs=[scalar]...  21.2 us
    pallas_call x1, Pallas kernels, own_block(): pl.pallas_call(own_kernel, in_specs=[scalar] * 2 + [off_chip] * 2, out_sp...  16.9 us
    pallas_call x2, Pallas kernels, last_block(): pl.pallas_call(functools.partial(last_kernel, inner), in_specs=[scalar] *...  7.78 us
    pallas_call x2, Pallas kernels, pieces_of(): pl.pallas_call(functools.partial(pieces_kernel, first), in_specs=[off_chi...  3.3 us
  transfers between devices with their start and end apart: 10, of which 6 were waited for; matrix products, arithmetic and copies ran while one was open for 0% of the time, Pallas kernels for 40%

profile of v5, /device:TPU:0, one launch (start us, length us, event | category | flops | bytes accessed | tf_op | source)
XLA Modules:
  0.0 116.3 jit_solution(9274578086177172523)
XLA Ops:
  0.6 1.3 %shard_map.60 = (bf16[256,1152]{1,0:T(8,128)(2,1)S(1)}, bf16[256,1152]{1,0:T(8,128)(2,1)S(1)}) custom-call(bf16[1024,1152]{1,0:T(8,128)(2,1)} %img_ref.5, bf16[1024,1152]{1,0:T(8,128)(2,1)} %txt_ref.5), custom_call_target="tpu_custom_call" | custom-call | bytes 1024 | tf_op jit(solution)/shard_map/pallas_call | solution.py:217
  1.9 1.7 %collective-permute-start = (bf16[256,1152]{1,0:T(8,128)(2,1)S(1)}, bf16[256,1152]{1,0:T(8,128)(2,1)S(1)}, u32[]{:S(2)}, u32[]{:S(2)}) collective-permute-start(bf16[256,1152]{1,0:T(8,128)(2,1)S(1)} %get-tuple-element.31.refs_0_), channel_id=1, source_target_pairs={{0,1},{1,0},{2,3},{3,2},{4,5},{5,4},{6,7},{7,6},{8,9},{9,8},{10,11... | collective-permute-start | bytes 1769480 | tf_op jit(solution)/shard_map/ppermute | solution.py:27
  3.7 7.0 %collective-permute-start.1 = (bf16[256,1152]{1,0:T(8,128)(2,1)S(1)}, bf16[256,1152]{1,0:T(8,128)(2,1)S(1)}, u32[]{:S(2)}, u32[]{:S(2)}) collective-permute-start(bf16[256,1152]{1,0:T(8,128)(2,1)S(1)} %shard_map.61), channel_id=1, source_target_pairs={{1,2},{2,1},{3,4},{4,3},{5,6},{6,5},{7,8},{8,7},{9,10},{10,9},{11,... | collective-permute-start | bytes 1769480 | tf_op jit(solution)/shard_map/ppermute | solution.py:27
  10.7 2.0 %shard_map.63 = (bf16[768,1152]{1,0:T(8,128)(2,1)S(1)}, bf16[768,1152]{1,0:T(8,128)(2,1)S(1)}) custom-call(bf16[1024,1152]{1,0:T(8,128)(2,1)} %img_ref.5, bf16[1024,1152]{1,0:T(8,128)(2,1)} %txt_ref.5, bf16[256,1152]{1,0:T(8,128)(2,1)S(1)} %get-tuple-element.31.refs_0_), custom_call_target="tpu_custom_call" | custom-call | bytes 1024 | tf_op jit(solution)/shard_map/pallas_call | solution.py:217
  12.7 0.1 collective-permute-start.2
  12.8 1.0 collective-permute-start.3
  15.1 16.9 %shard_map.59 = (bf16[1024,1152]{1,0:T(8,128)(2,1)S(1)}, bf16[1024,1152]{1,0:T(8,128)(2,1)S(1)}, f32[1024,1152]{1,0:T(8,128)S(1)}, f32[1024,1152]{1,0:T(8,128)S(...) custom-call(f32[1]{0:T(128)S(6)} %exp.3.temper_ref, ...), custom_call_target="tpu_custom_call" | custom-call | flops 38654705664 | bytes 4718592 | tf_op jit(solution)/shard_map/pallas_call | solution.py:270
  32.0 0.0 collective-permute-done.1.outer_ref
  32.0 0.0 collective-permute-done.inner_ref
  32.0 0.6 shard_map.62
  32.6 6.3 %collective-permute-start.5 = (bf16[256,1152]{1,0:T(8,128)(2,1)S(1)}, bf16[256,1152]{1,0:T(8,128)(2,1)S(1)}, u32[]{:S(2)}, u32[]{:S(2)}) collective-permute-start(bf16[256,1152]{1,0:T(8,128)(2,1)S(1)} %get-tuple-element.33.refs_0_), channel_id=1, source_target_pairs={{1,2},{2,1},{3,4},{4,3},{5,6},{6,5},{7,8},{8,7},{9,10},{10,9},{11,... | collective-permute-start | bytes 1769480 | tf_op jit(solution)/shard_map/ppermute | solution.py:27
  39.0 0.0 collective-permute-start.4
  39.0 17.2 %collective-permute-done.2.refs_2_ = bf16[768,1152]{1,0:T(8,128)(2,1)S(1)} collective-permute-done((bf16[768,1152]{1,0:T(8,128)(2,1)S(1)}, bf16[768,1152]{1,0:T(8,128)(2,1)S(1)}, u32[]{:S(2)}, u32[]{:S(2)}) %collective-permute-start.2) | collective-permute-done | bytes 1769504 | tf_op jit(solution)/shard_map/ppermute | solution.py:27
  56.1 6.2 %collective-permute-done.3.refs_3_ = bf16[768,1152]{1,0:T(8,128)(2,1)S(1)} collective-permute-done((bf16[768,1152]{1,0:T(8,128)(2,1)S(1)}, bf16[768,1152]{1,0:T(8,128)(2,1)S(1)}, u32[]{:S(2)}, u32[]{:S(2)}) %collective-permute-start.3) | collective-permute-done | bytes 1769504 | tf_op jit(solution)/shard_map/ppermute | solution.py:27
  62.4 2.1 %shard_map.64 = (bf16[1024,1152]{1,0:T(8,128)(2,1)S(1)}, bf16[1024,1152]{1,0:T(8,128)(2,1)S(1)}, bf16[512,1152]{1,0:T(8,128)(2,1)S(1)}, bf16[512,1152]{1,0:T(8,1...) custom-call(bf16[256,1152]{1,0:T(8,128)(2,1)S(1)} %get-tuple-element.33.refs_0_, ...), custom_call_target="tpu_custom_call" | custom-call | bytes 1024 | tf_op jit(solution)/shard_map/pallas_call | solution.py:243
  64.5 0.1 collective-permute-start.6
  64.6 7.4 %collective-permute-start.7 = (bf16[512,1152]{1,0:T(8,128)(2,1)S(1)}, bf16[512,1152]{1,0:T(8,128)(2,1)S(1)}, u32[]{:S(2)}, u32[]{:S(2)}) collective-permute-start(bf16[512,1152]{1,0:T(8,128)(2,1)S(1)} %get-tuple-element.46), channel_id=1, source_target_pairs={{1,2},{2,1},{3,4},{4,3},{5,6},{6,5},{7,8},{8,7},{9,10},{10,9},{11,... | collective-permute-start | bytes 3538952 | tf_op jit(solution)/shard_map/ppermute | solution.py:27
  72.0 5.9 %shard_map.65.refs_0_.sum_ref = f32[1024,1152]{1,0:T(8,128)S(1)} custom-call(f32[1]{0:T(128)S(6)} %exp.3.temper_ref, f32[1]{0:T(128)S(6)} %copy.33.offset_ref, bf16[1024,1152]{1,0:T(8,128)(2,1)S(1)} %get-tuple-element.28.own_unit, f32[1024,1152]{1,0:T(8,128)S(1)} %get-tuple-element.29.sum_ref, ...), custom_call_target="tpu_custom_call", output_to_operand_aliasing={{}: (3, {})} | custom-call | flops 7247757312 | bytes 4718592 | tf_op jit(solution)/shard_map/pallas_call | solution.py:285
  77.9 0.0 collective-permute-done.5.refs_4_
  77.9 0.0 collective-permute-done.4.refs_3_
  77.9 4.4 %collective-permute-start.8 = (bf16[256,1152]{1,0:T(8,128)(2,1)S(1)}, bf16[256,1152]{1,0:T(8,128)(2,1)S(1)}, u32[]{:S(2)}, u32[]{:S(2)}) collective-permute-start(bf16[256,1152]{1,0:T(8,128)(2,1)S(1)} %get-tuple-element.49), channel_id=1, source_target_pairs={{1,2},{2,1},{3,4},{4,3},{5,6},{6,5},{7,8},{8,7},{9,10},{10,9},{11,... | collective-permute-start | bytes 1769480 | tf_op jit(solution)/shard_map/ppermute | solution.py:27
  82.3 0.0 collective-permute-start.9
  82.3 5.9 %shard_map.67.sum_ref = f32[1024,1152]{1,0:T(8,128)S(1)} custom-call(f32[1]{0:T(128)S(6)} %exp.3.temper_ref, f32[1]{0:T(128)S(6)} %copy.33.offset_ref, bf16[1024,1152]{1,0:T(8,128)(2,1)S(1)} %get-tuple-element.41.own_unit, f32[1024,1152]{1,0:T(8,128)S(1)} %get-tuple-element.42.sum_ref, ...), custom_call_target="tpu_custom_call", output_to_operand_aliasing={{}: (3, {})} | custom-call | flops 7247757312 | bytes 4718592 | tf_op jit(solution)/shard_map/pallas_call | solution.py:285
  88.3 5.8 %collective-permute-done.6.middle = bf16[512,1152]{1,0:T(8,128)(2,1)S(1)} collective-permute-done((bf16[512,1152]{1,0:T(8,128)(2,1)S(1)}, bf16[512,1152]{1,0:T(8,128)(2,1)S(1)}, u32[]{:S(2)}, u32[]{:S(2)}) %collective-permute-start.6) | collective-permute-done | bytes 1179680 | tf_op jit(solution)/shard_map/ppermute | solution.py:27
  94.1 4.7 %shard_map.68.refs_0_.sum_ref = f32[1024,1152]{1,0:T(8,128)S(1)} custom-call(f32[1]{0:T(128)S(6)} %exp.3.temper_ref, f32[1]{0:T(128)S(6)} %copy.33.offset_ref, bf16[1024,1152]{1,0:T(8,128)(2,1)S(1)} %get-tuple-element.41.own_unit, f32[1024,1152]{1,0:T(8,128)S(1)} %shard_map.67.sum_ref, ...), custom_call_target="tpu_custom_call", output_to_operand_aliasing={{}: (3, {})} | custom-call | flops 9059696 | bytes 4718592 | tf_op jit(solution)/shard_map/pallas_call | solution.py:285
  98.7 1.6 %collective-permute-done.7.refs_1_ = bf16[512,1152]{1,0:T(8,128)(2,1)S(1)} collective-permute-done((bf16[512,1152]{1,0:T(8,128)(2,1)S(1)}, bf16[512,1152]{1,0:T(8,128)(2,1)S(1)}, u32[]{:S(2)}, u32[]{:S(2)}) %collective-permute-start.7) | collective-permute-done | bytes 1179680 | tf_op jit(solution)/shard_map/ppermute | solution.py:27
  100.3 4.7 %shard_map.70.refs_0_.sum_ref = f32[1024,1152]{1,0:T(8,128)S(1)} custom-call(f32[1]{0:T(128)S(6)} %exp.3.temper_ref, f32[1]{0:T(128)S(6)} %copy.33.offset_ref, bf16[1024,1152]{1,0:T(8,128)(2,1)S(1)} %get-tuple-element.28.own_unit, f32[1024,1152]{1,0:T(8,128)S(1)} %shard_map.65.refs_0_.sum_ref, ...), custom_call_target="tpu_custom_call", output_to_operand_aliasing={{}: (3, {})} | custom-call | flops 9059696 | bytes 4718592 | tf_op jit(solution)/shard_map/pallas_call | solution.py:285
  104.9 0.5 collective-permute-done.9.refs_1_
  105.5 3.9 %shard_map.72 = (f32[1024,1152]{1,0:T(8,128)}, f32[1024,1152]{1,0:T(8,128)}) custom-call(f32[1]{0:T(128)S(6)} %exp.3.temper_ref, f32[1]{0:T(128)S(6)} %copy.33.offset_ref, bf16[1024,1152]{1,0:T(8,128)(2,1)S(1)} %get-tuple-element.41.own_unit, f32[1024,1152]{1,0:T(8,128)S(1)} %shard_map.68.refs_0_.sum_ref, bf16[1024,1152]{1,0:T(8,128)(2,1)S(1)} %get-tuple-element.50.raw_ref, ...), custom_call_target="tpu_custom_call" | custom-call | flops 4831838208 | bytes 4718592 | tf_op jit(solution)/shard_map/pallas_call | solution.py:300
  109.4 2.9 %collective-permute-done.8.refs_0_ = bf16[256,1152]{1,0:T(8,128)(2,1)S(1)} collective-permute-done((bf16[256,1152]{1,0:T(8,128)(2,1)S(1)}, bf16[256,1152]{1,0:T(8,128)(2,1)S(1)}, u32[]{:S(2)}, u32[]{:S(2)}) %collective-permute-start.8) | collective-permute-done | bytes 589856 | tf_op jit(solution)/shard_map/ppermute | solution.py:27
  112.2 3.9 %shard_map.73 = (f32[1024,1152]{1,0:T(8,128)}, f32[1024,1152]{1,0:T(8,128)}) custom-call(f32[1]{0:T(128)S(6)} %exp.3.temper_ref, f32[1]{0:T(128)S(6)} %copy.33.offset_ref, bf16[1024,1152]{1,0:T(8,128)(2,1)S(1)} %get-tuple-element.28.own_unit, f32[1024,1152]{1,0:T(8,128)S(1)} %shard_map.70.refs_0_.sum_ref, ...), custom_call_target="tpu_custom_call", output_to_operand_aliasing={{0}: (7, {}), {1}: (8, {})} | custom-call | flops 4831838208 | bytes 4718592 | tf_op jit(solution)/shard_map/pallas_call | solution.py:300
  (4 shorter events, 0.0 us)
Async XLA Ops:
  1.9 30.1 %collective-permute-start = (bf16[256,1152]{1,0:T(8,128)(2,1)S(1)}, bf16[256,1152]{1,0:T(8,128)(2,1)S(1)}, u32[]{:S(2)}, u32[]{:S(2)}) collective-permute-start(bf16[256,1152]{1,0:T(8,128)(2,1)S(1)} %get-tuple-element.31.refs_0_), channel_id=1, source_target_pairs={{0,1},{1,0},{2,3},{3,2},{4,5},{5,4},{6,7},{7,6},{8,9},{9,8},{10,11... | collective-permute-start | bytes 1769480 | tf_op jit(solution)/shard_map/ppermute | solution.py:27
  3.7 28.3 %collective-permute-start.1 = (bf16[256,1152]{1,0:T(8,128)(2,1)S(1)}, bf16[256,1152]{1,0:T(8,128)(2,1)S(1)}, u32[]{:S(2)}, u32[]{:S(2)}) collective-permute-start(bf16[256,1152]{1,0:T(8,128)(2,1)S(1)} %shard_map.61), channel_id=1, source_target_pairs={{1,2},{2,1},{3,4},{4,3},{5,6},{6,5},{7,8},{8,7},{9,10},{10,9},{11,... | collective-permute-start | bytes 1769480 | tf_op jit(solution)/shard_map/ppermute | solution.py:27
  12.7 43.4 %collective-permute-start.2 = (bf16[768,1152]{1,0:T(8,128)(2,1)S(1)}, bf16[768,1152]{1,0:T(8,128)(2,1)S(1)}, u32[]{:S(2)}, u32[]{:S(2)}) collective-permute-start(bf16[768,1152]{1,0:T(8,128)(2,1)S(1)} %get-tuple-element.35), channel_id=1, source_target_pairs={{0,1},{1,0},{2,3},{3,2},{4,5},{5,4},{6,7},{7,6},{8,9},{9,8},{10,11... | collective-permute-start | bytes 5308424 | tf_op jit(solution)/shard_map/ppermute | solution.py:27
  12.8 49.6 %collective-permute-start.3 = (bf16[768,1152]{1,0:T(8,128)(2,1)S(1)}, bf16[768,1152]{1,0:T(8,128)(2,1)S(1)}, u32[]{:S(2)}, u32[]{:S(2)}) collective-permute-start(bf16[768,1152]{1,0:T(8,128)(2,1)S(1)} %get-tuple-element.36), channel_id=1, source_target_pairs={{1,2},{2,1},{3,4},{4,3},{5,6},{6,5},{7,8},{8,7},{9,10},{10,9},{11,... | collective-permute-start | bytes 5308424 | tf_op jit(solution)/shard_map/ppermute | solution.py:27
  32.6 45.3 %collective-permute-start.5 = (bf16[256,1152]{1,0:T(8,128)(2,1)S(1)}, bf16[256,1152]{1,0:T(8,128)(2,1)S(1)}, u32[]{:S(2)}, u32[]{:S(2)}) collective-permute-start(bf16[256,1152]{1,0:T(8,128)(2,1)S(1)} %get-tuple-element.33.refs_0_), channel_id=1, source_target_pairs={{1,2},{2,1},{3,4},{4,3},{5,6},{6,5},{7,8},{8,7},{9,10},{10,9},{11,... | collective-permute-start | bytes 1769480 | tf_op jit(solution)/shard_map/ppermute | solution.py:27
  39.0 39.0 %collective-permute-start.4 = (bf16[256,1152]{1,0:T(8,128)(2,1)S(1)}, bf16[256,1152]{1,0:T(8,128)(2,1)S(1)}, u32[]{:S(2)}, u32[]{:S(2)}) collective-permute-start(bf16[256,1152]{1,0:T(8,128)(2,1)S(1)} %get-tuple-element.34.refs_1_), channel_id=1, source_target_pairs={{0,1},{1,0},{2,3},{3,2},{4,5},{5,4},{6,7},{7,6},{8,9},{9,8},{10,11... | collective-permute-start | bytes 1769480 | tf_op jit(solution)/shard_map/ppermute | solution.py:27
  64.5 29.6 %collective-permute-start.6 = (bf16[512,1152]{1,0:T(8,128)(2,1)S(1)}, bf16[512,1152]{1,0:T(8,128)(2,1)S(1)}, u32[]{:S(2)}, u32[]{:S(2)}) collective-permute-start(bf16[512,1152]{1,0:T(8,128)(2,1)S(1)} %get-tuple-element.45), channel_id=1, source_target_pairs={{0,1},{1,0},{2,3},{3,2},{4,5},{5,4},{6,7},{7,6},{8,9},{9,8},{10,11... | collective-permute-start | bytes 3538952 | tf_op jit(solution)/shard_map/ppermute | solution.py:27
  64.6 35.7 %collective-permute-start.7 = (bf16[512,1152]{1,0:T(8,128)(2,1)S(1)}, bf16[512,1152]{1,0:T(8,128)(2,1)S(1)}, u32[]{:S(2)}, u32[]{:S(2)}) collective-permute-start(bf16[512,1152]{1,0:T(8,128)(2,1)S(1)} %get-tuple-element.46), channel_id=1, source_target_pairs={{1,2},{2,1},{3,4},{4,3},{5,6},{6,5},{7,8},{8,7},{9,10},{10,9},{11,... | collective-permute-start | bytes 3538952 | tf_op jit(solution)/shard_map/ppermute | solution.py:27
  77.9 34.3 %collective-permute-start.8 = (bf16[256,1152]{1,0:T(8,128)(2,1)S(1)}, bf16[256,1152]{1,0:T(8,128)(2,1)S(1)}, u32[]{:S(2)}, u32[]{:S(2)}) collective-permute-start(bf16[256,1152]{1,0:T(8,128)(2,1)S(1)} %get-tuple-element.49), channel_id=1, source_target_pairs={{1,2},{2,1},{3,4},{4,3},{5,6},{6,5},{7,8},{8,7},{9,10},{10,9},{11,... | collective-permute-start | bytes 1769480 | tf_op jit(solution)/shard_map/ppermute | solution.py:27
  82.3 23.1 %collective-permute-start.9 = (bf16[256,1152]{1,0:T(8,128)(2,1)S(1)}, bf16[256,1152]{1,0:T(8,128)(2,1)S(1)}, u32[]{:S(2)}, u32[]{:S(2)}) collective-permute-start(bf16[256,1152]{1,0:T(8,128)(2,1)S(1)} %get-tuple-element.51), channel_id=1, source_target_pairs={{0,1},{1,0},{2,3},{3,2},{4,5},{5,4},{6,7},{7,6},{8,9},{9,8},{10,11... | collective-permute-start | bytes 1769480 | tf_op jit(solution)/shard_map/ppermute | solution.py:27

commit v6 on v5

--- a/solution.py
+++ b/solution.py
@@ -11,9 +11,9 @@
 epsilon = 1e-06
 axes = ("grp", "dev")
 start = 256
-split = 768
+split = 832
 tile = 256
-last_tiles = (128, 256, 256, 256, 128)
+last_tiles = (128, 256, 256, 256, 64, 64)
 lanes = 128
 
 
@@ -167,10 +167,15 @@
 
         def finish(rows, total):
             raw = raw_ref[rows, :].astype(jnp.float32)
-            inverse = inverse_ref[rows, :1]
+            inverse = inverse_ref[rows, :]
             scale = temper * inverse
-            along = jnp.sum(raw * total, axis=1, keepdims=True)
-            ready[rows, :] = scale * total - (scale * inverse * inverse * along) * raw
+            groups = [slice(low, low + lanes) for low in range(0, raw.shape[1], lanes)]
+            along = jnp.sum(
+                sum(raw[:, group] * total[:, group] for group in groups), axis=1, keepdims=True
+            )
+            back = scale * inverse * inverse * along
+            for group in groups:
+                ready[rows, group] = scale * total[:, group] - back * raw[:, group]
             copies.append(
                 pltpu.make_async_copy(ready.at[rows, :], into.at[rows, :], sems.at[len(copies)])
             )

time: 116 us -> 118 us (1.017)
  Pallas kernels: 51.8 us -> 55 us
  waiting for transfers between devices: 34.1 us -> 32.5 us
    pallas_call x4, Pallas kernels: 21.2 us -> 24.3 us  [more_block(): pl.pallas_call(far_kernel if several else near_kernel, in_specs=[scalar]...]
    ppermute x10, waiting for transfers between devices: 34.1 us -> 32.5 us  [exchanged(): return lax.ppermute(value, axes, pairs)]
  transfers between devices with their start and end apart: 10 -> 10, of which waited for: 6 -> 4; matrix products, arithmetic and copies ran while one was open for 0% -> 0% of each run, Pallas kernels for 40% -> 42%
where the time goes in v6:
time: 118 us
  Pallas kernels  55 us (47%)
  waiting for transfers between devices  32.5 us (28%)
  starting transfers between devices  28.1 us (24%)
  between operations  2.3 us (2%)
    ppermute x10, waiting for transfers between devices, exchanged(): return lax.ppermute(value, axes, pairs)  32.5 us
    ppermute x10, starting transfers between devices, exchanged(): return lax.ppermute(value, axes, pairs)  28.1 us
    pallas_call x4, Pallas kernels, more_block(): pl.pallas_call(far_kernel if several else near_kernel, in_specs=[scalar]...  24.3 us
    pallas_call x1, Pallas kernels, own_block(): pl.pallas_call(own_kernel, in_specs=[scalar] * 2 + [off_chip] * 2, out_sp...  16.9 us
    pallas_call x2, Pallas kernels, last_block(): pl.pallas_call(functools.partial(last_kernel, inner), in_specs=[scalar] *...  7.9 us
    pallas_call x2, Pallas kernels, pieces_of(): pl.pallas_call(functools.partial(pieces_kernel, first), in_specs=[off_chi...  3.3 us
  transfers between devices with their start and end apart: 10, of which 4 were waited for; matrix products, arithmetic and copies ran while one was open for 0% of the time, Pallas kernels for 42%

profile of v6, /device:TPU:0, one launch (start us, length us, event | category | flops | bytes accessed | tf_op | source)
XLA Modules:
  0.0 117.9 jit_solution(1197183691719181105)
XLA Ops:
  0.6 1.3 %shard_map.60 = (bf16[256,1152]{1,0:T(8,128)(2,1)S(1)}, bf16[256,1152]{1,0:T(8,128)(2,1)S(1)}) custom-call(bf16[1024,1152]{1,0:T(8,128)(2,1)} %img_ref.5, bf16[1024,1152]{1,0:T(8,128)(2,1)} %txt_ref.5), custom_call_target="tpu_custom_call" | custom-call | bytes 1024 | tf_op jit(solution)/shard_map/pallas_call | solution.py:222
  1.9 1.7 %collective-permute-start = (bf16[256,1152]{1,0:T(8,128)(2,1)S(1)}, bf16[256,1152]{1,0:T(8,128)(2,1)S(1)}, u32[]{:S(2)}, u32[]{:S(2)}) collective-permute-start(bf16[256,1152]{1,0:T(8,128)(2,1)S(1)} %get-tuple-element.31.refs_0_), channel_id=1, source_target_pairs={{0,1},{1,0},{2,3},{3,2},{4,5},{5,4},{6,7},{7,6},{8,9},{9,8},{10,11... | collective-permute-start | bytes 1769480 | tf_op jit(solution)/shard_map/ppermute | solution.py:27
  3.7 7.0 %collective-permute-start.1 = (bf16[256,1152]{1,0:T(8,128)(2,1)S(1)}, bf16[256,1152]{1,0:T(8,128)(2,1)S(1)}, u32[]{:S(2)}, u32[]{:S(2)}) collective-permute-start(bf16[256,1152]{1,0:T(8,128)(2,1)S(1)} %shard_map.61), channel_id=1, source_target_pairs={{1,2},{2,1},{3,4},{4,3},{5,6},{6,5},{7,8},{8,7},{9,10},{10,9},{11,... | collective-permute-start | bytes 1769480 | tf_op jit(solution)/shard_map/ppermute | solution.py:27
  10.7 2.0 %shard_map.63 = (bf16[768,1152]{1,0:T(8,128)(2,1)S(1)}, bf16[768,1152]{1,0:T(8,128)(2,1)S(1)}) custom-call(bf16[1024,1152]{1,0:T(8,128)(2,1)} %img_ref.5, bf16[1024,1152]{1,0:T(8,128)(2,1)} %txt_ref.5, bf16[256,1152]{1,0:T(8,128)(2,1)S(1)} %get-tuple-element.31.refs_0_), custom_call_target="tpu_custom_call" | custom-call | bytes 1024 | tf_op jit(solution)/shard_map/pallas_call | solution.py:222
  12.7 0.1 collective-permute-start.2
  12.8 1.0 collective-permute-start.3
  15.1 16.9 %shard_map.59 = (bf16[1024,1152]{1,0:T(8,128)(2,1)S(1)}, bf16[1024,1152]{1,0:T(8,128)(2,1)S(1)}, f32[1024,1152]{1,0:T(8,128)S(1)}, f32[1024,1152]{1,0:T(8,128)S(...) custom-call(f32[1]{0:T(128)S(6)} %exp.3.temper_ref, ...), custom_call_target="tpu_custom_call" | custom-call | flops 38654705664 | bytes 4718592 | tf_op jit(solution)/shard_map/pallas_call | solution.py:275
  32.0 0.0 collective-permute-done.1.outer_ref
  32.0 0.0 collective-permute-done.inner_ref
  32.0 0.6 shard_map.62
  32.6 6.3 %collective-permute-start.5 = (bf16[256,1152]{1,0:T(8,128)(2,1)S(1)}, bf16[256,1152]{1,0:T(8,128)(2,1)S(1)}, u32[]{:S(2)}, u32[]{:S(2)}) collective-permute-start(bf16[256,1152]{1,0:T(8,128)(2,1)S(1)} %get-tuple-element.33.refs_0_), channel_id=1, source_target_pairs={{1,2},{2,1},{3,4},{4,3},{5,6},{6,5},{7,8},{8,7},{9,10},{10,9},{11,... | collective-permute-start | bytes 1769480 | tf_op jit(solution)/shard_map/ppermute | solution.py:27
  39.0 0.0 collective-permute-start.4
  39.0 17.2 %collective-permute-done.2.refs_2_ = bf16[768,1152]{1,0:T(8,128)(2,1)S(1)} collective-permute-done((bf16[768,1152]{1,0:T(8,128)(2,1)S(1)}, bf16[768,1152]{1,0:T(8,128)(2,1)S(1)}, u32[]{:S(2)}, u32[]{:S(2)}) %collective-permute-start.2) | collective-permute-done | bytes 1769504 | tf_op jit(solution)/shard_map/ppermute | solution.py:27
  56.1 6.2 %collective-permute-done.3.refs_3_ = bf16[768,1152]{1,0:T(8,128)(2,1)S(1)} collective-permute-done((bf16[768,1152]{1,0:T(8,128)(2,1)S(1)}, bf16[768,1152]{1,0:T(8,128)(2,1)S(1)}, u32[]{:S(2)}, u32[]{:S(2)}) %collective-permute-start.3) | collective-permute-done | bytes 1769504 | tf_op jit(solution)/shard_map/ppermute | solution.py:27
  62.4 2.1 %shard_map.64 = (bf16[1024,1152]{1,0:T(8,128)(2,1)S(1)}, bf16[1024,1152]{1,0:T(8,128)(2,1)S(1)}, bf16[576,1152]{1,0:T(8,128)(2,1)S(1)}, bf16[576,1152]{1,0:T(8,1...) custom-call(bf16[256,1152]{1,0:T(8,128)(2,1)S(1)} %get-tuple-element.33.refs_0_, ...), custom_call_target="tpu_custom_call" | custom-call | bytes 1024 | tf_op jit(solution)/shard_map/pallas_call | solution.py:248
  64.5 0.1 collective-permute-start.6
  64.6 7.4 %collective-permute-start.7 = (bf16[576,1152]{1,0:T(8,128)(2,1)S(1)}, bf16[576,1152]{1,0:T(8,128)(2,1)S(1)}, u32[]{:S(2)}, u32[]{:S(2)}) collective-permute-start(bf16[576,1152]{1,0:T(8,128)(2,1)S(1)} %get-tuple-element.46), channel_id=1, source_target_pairs={{1,2},{2,1},{3,4},{4,3},{5,6},{6,5},{7,8},{8,7},{9,10},{10,9},{11,... | collective-permute-start | bytes 3981320 | tf_op jit(solution)/shard_map/ppermute | solution.py:27
  72.0 5.9 %shard_map.65.refs_0_.sum_ref = f32[1024,1152]{1,0:T(8,128)S(1)} custom-call(f32[1]{0:T(128)S(6)} %exp.3.temper_ref, f32[1]{0:T(128)S(6)} %copy.33.offset_ref, bf16[1024,1152]{1,0:T(8,128)(2,1)S(1)} %get-tuple-element.28.own_unit, f32[1024,1152]{1,0:T(8,128)S(1)} %get-tuple-element.29.sum_ref, ...), custom_call_target="tpu_custom_call", output_to_operand_aliasing={{}: (3, {})} | custom-call | flops 7247757312 | bytes 4718592 | tf_op jit(solution)/shard_map/pallas_call | solution.py:290
  77.9 0.0 collective-permute-done.5.refs_4_
  77.9 0.0 collective-permute-done.4.refs_3_
  77.9 4.4 %collective-permute-start.8 = (bf16[192,1152]{1,0:T(8,128)(2,1)S(1)}, bf16[192,1152]{1,0:T(8,128)(2,1)S(1)}, u32[]{:S(2)}, u32[]{:S(2)}) collective-permute-start(bf16[192,1152]{1,0:T(8,128)(2,1)S(1)} %get-tuple-element.49), channel_id=1, source_target_pairs={{1,2},{2,1},{3,4},{4,3},{5,6},{6,5},{7,8},{8,7},{9,10},{10,9},{11,... | collective-permute-start | bytes 1327112 | tf_op jit(solution)/shard_map/ppermute | solution.py:27
  82.3 0.0 collective-permute-start.9
  82.3 5.9 %shard_map.67.sum_ref = f32[1024,1152]{1,0:T(8,128)S(1)} custom-call(f32[1]{0:T(128)S(6)} %exp.3.temper_ref, f32[1]{0:T(128)S(6)} %copy.33.offset_ref, bf16[1024,1152]{1,0:T(8,128)(2,1)S(1)} %get-tuple-element.41.own_unit, f32[1024,1152]{1,0:T(8,128)S(1)} %get-tuple-element.42.sum_ref, ...), custom_call_target="tpu_custom_call", output_to_operand_aliasing={{}: (3, {})} | custom-call | flops 7247757312 | bytes 4718592 | tf_op jit(solution)/shard_map/pallas_call | solution.py:290
  88.3 8.9 %collective-permute-done.6.middle = bf16[576,1152]{1,0:T(8,128)(2,1)S(1)} collective-permute-done((bf16[576,1152]{1,0:T(8,128)(2,1)S(1)}, bf16[576,1152]{1,0:T(8,128)(2,1)S(1)}, u32[]{:S(2)}, u32[]{:S(2)}) %collective-permute-start.6) | collective-permute-done | bytes 1327136 | tf_op jit(solution)/shard_map/ppermute | solution.py:27
  97.2 6.1 %shard_map.68.refs_0_.sum_ref = f32[1024,1152]{1,0:T(8,128)S(1)} custom-call(f32[1]{0:T(128)S(6)} %exp.3.temper_ref, f32[1]{0:T(128)S(6)} %copy.33.offset_ref, bf16[1024,1152]{1,0:T(8,128)(2,1)S(1)} %get-tuple-element.41.own_unit, f32[1024,1152]{1,0:T(8,128)S(1)} %shard_map.67.sum_ref, ...), custom_call_target="tpu_custom_call", output_to_operand_aliasing={{}: (3, {})} | custom-call | flops 9814671 | bytes 4718592 | tf_op jit(solution)/shard_map/pallas_call | solution.py:290
  103.3 0.1 collective-permute-done.7.refs_1_
  103.4 6.3 %shard_map.70.refs_0_.sum_ref = f32[1024,1152]{1,0:T(8,128)S(1)} custom-call(f32[1]{0:T(128)S(6)} %exp.3.temper_ref, f32[1]{0:T(128)S(6)} %copy.33.offset_ref, bf16[1024,1152]{1,0:T(8,128)(2,1)S(1)} %get-tuple-element.28.own_unit, f32[1024,1152]{1,0:T(8,128)S(1)} %shard_map.65.refs_0_.sum_ref, ...), custom_call_target="tpu_custom_call", output_to_operand_aliasing={{}: (3, {})} | custom-call | flops 9814671 | bytes 4718592 | tf_op jit(solution)/shard_map/pallas_call | solution.py:290
  109.7 0.0 collective-permute-done.9.refs_1_
  109.8 4.0 %shard_map.72 = (f32[1024,1152]{1,0:T(8,128)}, f32[1024,1152]{1,0:T(8,128)}) custom-call(f32[1]{0:T(128)S(6)} %exp.3.temper_ref, f32[1]{0:T(128)S(6)} %copy.33.offset_ref, bf16[1024,1152]{1,0:T(8,128)(2,1)S(1)} %get-tuple-element.41.own_unit, f32[1024,1152]{1,0:T(8,128)S(1)} %shard_map.68.refs_0_.sum_ref, bf16[1024,1152]{1,0:T(8,128)(2,1)S(1)} %get-tuple-element.50.raw_ref, ...), custom_call_target="tpu_custom_call" | custom-call | flops 3623878656 | bytes 4718592 | tf_op jit(solution)/shard_map/pallas_call | solution.py:305
  113.7 0.0 collective-permute-done.8.refs_0_
  113.7 4.0 %shard_map.73 = (f32[1024,1152]{1,0:T(8,128)}, f32[1024,1152]{1,0:T(8,128)}) custom-call(f32[1]{0:T(128)S(6)} %exp.3.temper_ref, f32[1]{0:T(128)S(6)} %copy.33.offset_ref, bf16[1024,1152]{1,0:T(8,128)(2,1)S(1)} %get-tuple-element.28.own_unit, f32[1024,1152]{1,0:T(8,128)S(1)} %shard_map.70.refs_0_.sum_ref, ...), custom_call_target="tpu_custom_call", output_to_operand_aliasing={{0}: (7, {}), {1}: (8, {})} | custom-call | flops 3623878656 | bytes 4718592 | tf_op jit(solution)/shard_map/pallas_call | solution.py:305
  (4 shorter events, 0.0 us)
Async XLA Ops:
  1.9 30.1 %collective-permute-start = (bf16[256,1152]{1,0:T(8,128)(2,1)S(1)}, bf16[256,1152]{1,0:T(8,128)(2,1)S(1)}, u32[]{:S(2)}, u32[]{:S(2)}) collective-permute-start(bf16[256,1152]{1,0:T(8,128)(2,1)S(1)} %get-tuple-element.31.refs_0_), channel_id=1, source_target_pairs={{0,1},{1,0},{2,3},{3,2},{4,5},{5,4},{6,7},{7,6},{8,9},{9,8},{10,11... | collective-permute-start | bytes 1769480 | tf_op jit(solution)/shard_map/ppermute | solution.py:27
  3.7 28.3 %collective-permute-start.1 = (bf16[256,1152]{1,0:T(8,128)(2,1)S(1)}, bf16[256,1152]{1,0:T(8,128)(2,1)S(1)}, u32[]{:S(2)}, u32[]{:S(2)}) collective-permute-start(bf16[256,1152]{1,0:T(8,128)(2,1)S(1)} %shard_map.61), channel_id=1, source_target_pairs={{1,2},{2,1},{3,4},{4,3},{5,6},{6,5},{7,8},{8,7},{9,10},{10,9},{11,... | collective-permute-start | bytes 1769480 | tf_op jit(solution)/shard_map/ppermute | solution.py:27
  12.7 43.4 %collective-permute-start.2 = (bf16[768,1152]{1,0:T(8,128)(2,1)S(1)}, bf16[768,1152]{1,0:T(8,128)(2,1)S(1)}, u32[]{:S(2)}, u32[]{:S(2)}) collective-permute-start(bf16[768,1152]{1,0:T(8,128)(2,1)S(1)} %get-tuple-element.35), channel_id=1, source_target_pairs={{0,1},{1,0},{2,3},{3,2},{4,5},{5,4},{6,7},{7,6},{8,9},{9,8},{10,11... | collective-permute-start | bytes 5308424 | tf_op jit(solution)/shard_map/ppermute | solution.py:27
  12.8 49.6 %collective-permute-start.3 = (bf16[768,1152]{1,0:T(8,128)(2,1)S(1)}, bf16[768,1152]{1,0:T(8,128)(2,1)S(1)}, u32[]{:S(2)}, u32[]{:S(2)}) collective-permute-start(bf16[768,1152]{1,0:T(8,128)(2,1)S(1)} %get-tuple-element.36), channel_id=1, source_target_pairs={{1,2},{2,1},{3,4},{4,3},{5,6},{6,5},{7,8},{8,7},{9,10},{10,9},{11,... | collective-permute-start | bytes 5308424 | tf_op jit(solution)/shard_map/ppermute | solution.py:27
  32.6 45.3 %collective-permute-start.5 = (bf16[256,1152]{1,0:T(8,128)(2,1)S(1)}, bf16[256,1152]{1,0:T(8,128)(2,1)S(1)}, u32[]{:S(2)}, u32[]{:S(2)}) collective-permute-start(bf16[256,1152]{1,0:T(8,128)(2,1)S(1)} %get-tuple-element.33.refs_0_), channel_id=1, source_target_pairs={{1,2},{2,1},{3,4},{4,3},{5,6},{6,5},{7,8},{8,7},{9,10},{10,9},{11,... | collective-permute-start | bytes 1769480 | tf_op jit(solution)/shard_map/ppermute | solution.py:27
  39.0 39.0 %collective-permute-start.4 = (bf16[256,1152]{1,0:T(8,128)(2,1)S(1)}, bf16[256,1152]{1,0:T(8,128)(2,1)S(1)}, u32[]{:S(2)}, u32[]{:S(2)}) collective-permute-start(bf16[256,1152]{1,0:T(8,128)(2,1)S(1)} %get-tuple-element.34.refs_1_), channel_id=1, source_target_pairs={{0,1},{1,0},{2,3},{3,2},{4,5},{5,4},{6,7},{7,6},{8,9},{9,8},{10,11... | collective-permute-start | bytes 1769480 | tf_op jit(solution)/shard_map/ppermute | solution.py:27
  64.5 32.7 %collective-permute-start.6 = (bf16[576,1152]{1,0:T(8,128)(2,1)S(1)}, bf16[576,1152]{1,0:T(8,128)(2,1)S(1)}, u32[]{:S(2)}, u32[]{:S(2)}) collective-permute-start(bf16[576,1152]{1,0:T(8,128)(2,1)S(1)} %get-tuple-element.45), channel_id=1, source_target_pairs={{0,1},{1,0},{2,3},{3,2},{4,5},{5,4},{6,7},{7,6},{8,9},{9,8},{10,11... | collective-permute-start | bytes 3981320 | tf_op jit(solution)/shard_map/ppermute | solution.py:27
  64.6 38.9 %collective-permute-start.7 = (bf16[576,1152]{1,0:T(8,128)(2,1)S(1)}, bf16[576,1152]{1,0:T(8,128)(2,1)S(1)}, u32[]{:S(2)}, u32[]{:S(2)}) collective-permute-start(bf16[576,1152]{1,0:T(8,128)(2,1)S(1)} %get-tuple-element.46), channel_id=1, source_target_pairs={{1,2},{2,1},{3,4},{4,3},{5,6},{6,5},{7,8},{8,7},{9,10},{10,9},{11,... | collective-permute-start | bytes 3981320 | tf_op jit(solution)/shard_map/ppermute | solution.py:27
  77.9 35.8 %collective-permute-start.8 = (bf16[192,1152]{1,0:T(8,128)(2,1)S(1)}, bf16[192,1152]{1,0:T(8,128)(2,1)S(1)}, u32[]{:S(2)}, u32[]{:S(2)}) collective-permute-start(bf16[192,1152]{1,0:T(8,128)(2,1)S(1)} %get-tuple-element.49), channel_id=1, source_target_pairs={{1,2},{2,1},{3,4},{4,3},{5,6},{6,5},{7,8},{8,7},{9,10},{10,9},{11,... | collective-permute-start | bytes 1327112 | tf_op jit(solution)/shard_map/ppermute | solution.py:27
  82.3 27.4 %collective-permute-start.9 = (bf16[192,1152]{1,0:T(8,128)(2,1)S(1)}, bf16[192,1152]{1,0:T(8,128)(2,1)S(1)}, u32[]{:S(2)}, u32[]{:S(2)}) collective-permute-start(bf16[192,1152]{1,0:T(8,128)(2,1)S(1)} %get-tuple-element.51), channel_id=1, source_target_pairs={{0,1},{1,0},{2,3},{3,2},{4,5},{5,4},{6,7},{7,6},{8,9},{9,8},{10,11... | collective-permute-start | bytes 1327112 | tf_op jit(solution)/shard_map/ppermute | solution.py:27
